TPU v7x, 256 devices: a whole 4x4x8 slice. The times are simulated.
256 devices in a mesh: fsdp: 32 (over z, y), tensor: 8 (over x, core).
Axes of the slice: x: 4, y: 4, z: 8, core: 2. Of those that a mesh axis runs over, the one named last changes fastest.
Arguments:
- momentum: float32 [2, 4096, 1536], P(None, 'fsdp', 'tensor'), may hold values from -90 to 90
- grad: bfloat16 [2, 4096, 1536], P(None, 'fsdp', 'tensor'), may hold values from -3 to 3
- basis: float32 [2, 1536, 512], P(None, 'tensor'), may hold values from -6 to 6
Outputs:
- new_momentum: float32 [2, 4096, 1536], P(None, 'fsdp', 'tensor')
- new_basis: float32 [2, 1536, 512], P(None, 'tensor')
- update: bfloat16 [2, 4096, 1536], P(None, 'fsdp', 'tensor')
All inputs are finite; a program needn't handle non-finite values.
Results may differ from a plain program's by a relative error of at most 0.0011.
Values sent between devices are 32-bit elements; how exact they have to be, the bound alone decides.
A program may use at most 64 MiB of HBM per device.

v0:
```python
import math

import jax
import jax.numpy as jnp
from jax import lax
from jax.sharding import PartitionSpec as P

D = 4096
FF = 1536
RANK = 512


def on_device(momentum, grad, basis):
    highest = lax.Precision.HIGHEST
    blended = momentum + grad.astype(jnp.float32)
    partial_proj = jnp.einsum("mdf,mfr->mdr", blended, basis, precision=highest)
    projected = lax.psum(partial_proj, "tensor")
    local_gram = jnp.einsum("mdr,mds->mrs", projected, projected, precision=highest)
    gram = lax.psum(local_gram, "fsdp")
    factor = jnp.linalg.cholesky(gram)
    ortho = lax.linalg.triangular_solve(
        factor, projected, left_side=False, lower=True, transpose_a=True
    )
    partial_coeffs = jnp.einsum("mdf,mdr->mfr", blended, ortho, precision=highest)
    coeffs = lax.psum(partial_coeffs, "fsdp")
    squares = lax.psum(jnp.sum(coeffs * coeffs, axis=1), "tensor")
    new_basis = coeffs * lax.rsqrt(squares + 1e-06)[:, None, :]
    new_momentum = blended - 0.05 * jnp.einsum("mdr,mfr->mdf", ortho, coeffs, precision=highest)
    factor_scale = math.sqrt(D * FF / RANK)
    update = (
        factor_scale * jnp.einsum("mdr,mfr->mdf", ortho, new_basis, precision=highest)
    ).astype(jnp.bfloat16)
    return (new_momentum, new_basis, update)


def solution(mesh):
    in_specs = (P(None, "fsdp", "tensor"), P(None, "fsdp", "tensor"), P(None, "tensor", None))
    out_specs = (P(None, "fsdp", "tensor"), P(None, "tensor", None), P(None, "fsdp", "tensor"))
    return jax.shard_map(
        on_device, mesh=mesh, in_specs=in_specs, out_specs=out_specs, check_vma=False
    )
```

profile of v0, /device:TPU:1, one launch (start us, length us, event | category | flops | bytes accessed | tf_op | source)
XLA Modules:
  0.0 690.5 jit_solution(1288309736466009821)
XLA Ops:
  7.2 0.0 all-reduce.5.cloned.1.call-start
  7.2 1.1 copy-done
  8.3 2.5 fusion.31
  10.8 0.0 all-reduce.7.cloned.1.call-start
  10.9 67.6 %all-reduce.5.cloned.1.call-done = f32[2,128,512]{2,1,0:T(8,128)} async-done(((f32[2,128,512]{2,1,0:T(8,128)}), f32[2,128,512]{2,1,0:T(8,128)}) %all-reduce.5.cloned.1.call-update) | async-done | bytes 524304 | tf_op jit(solution)/shard_map/psum | solution.py:17
  78.5 4.3 fusion.38
  82.8 0.5 all-reduce.9.cloned.1.call-start
  83.4 0.6 iota_multiply_fusion
  83.9 0.6 iota_compare_fusion.2
  84.6 0.8 iota_compare_fusion
  85.4 148.8 %all-reduce.7.cloned.1.call-done = f32[2,512,512]{1,2,0:T(8,128)} async-done(((f32[2,512,512]{1,2,0:T(8,128)}), f32[2,512,512]{1,2,0:T(8,128)}) %all-reduce.7.cloned.1.call-update) | async-done | bytes 2097168 | tf_op jit(solution)/shard_map/psum | solution.py:19
  234.1 3.0 copy.25
  237.2 2.1 fusion
  239.3 1.3 copy-done.3
  240.6 23.5 %custom-call.34 = f32[2,128,128]{2,1,0:T(8,128)S(1)} custom-call(f32[2,128,128]{2,1,0:T(8,128)S(1)} %cholesky.274), custom_call_target="Cholesky" | custom-call | tf_op jit(solution)/shard_map/jit(cholesky)/cholesky | solution.py:20
  264.1 19.7 %custom-call.35 = f32[2,1,128,128]{2,3,1,0:T(8,128)S(1)} custom-call(f32[2,1,128,128]{3,2,1,0:T(8,128)S(1)} %select_bitcast_fusion.2), custom_call_target="InvertDiagBlocksLowerTriangular" | custom-call | tf_op jit(solution)/shard_map/jit(cholesky)/cholesky | solution.py:20
  283.8 0.3 cholesky.234
  284.0 1.5 constant_dynamic-update-slice_fusion.3
  285.6 1.5 convolution_subtract_fusion
  287.1 0.7 cholesky.278
  287.7 24.3 %custom-call.36 = f32[2,128,128]{2,1,0:T(8,128)S(1)} custom-call(f32[2,128,128]{2,1,0:T(8,128)} %cholesky.278), custom_call_target="Cholesky" | custom-call | tf_op jit(solution)/shard_map/jit(cholesky)/cholesky | solution.py:20
  312.0 0.7 select_bitcast_fusion.1
  312.7 21.2 %custom-call.37 = f32[2,1,128,128]{2,3,1,0:T(8,128)} custom-call(f32[2,1,128,128]{3,2,1,0:T(8,128)} %get-tuple-element.28), custom_call_target="InvertDiagBlocksLowerTriangular" | custom-call | tf_op jit(solution)/shard_map/jit(cholesky)/cholesky | solution.py:20
  333.9 1.3 convolution_dynamic-update-slice_fusion
  335.2 1.6 convolution_subtract_fusion.1
  336.8 0.7 cholesky.283
  337.4 24.3 %custom-call.38 = f32[2,128,128]{2,1,0:T(8,128)S(1)} custom-call(f32[2,128,128]{2,1,0:T(8,128)} %cholesky.283), custom_call_target="Cholesky" | custom-call | tf_op jit(solution)/shard_map/jit(cholesky)/cholesky | solution.py:20
  361.7 0.7 select_bitcast_fusion
  362.4 21.1 %custom-call.39 = f32[2,1,128,128]{2,3,1,0:T(8,128)} custom-call(f32[2,1,128,128]{3,2,1,0:T(8,128)} %get-tuple-element.26), custom_call_target="InvertDiagBlocksLowerTriangular" | custom-call | tf_op jit(solution)/shard_map/jit(cholesky)/cholesky | solution.py:20
  383.5 1.2 convolution_dynamic-update-slice_fusion.1
  384.7 1.5 convolution_subtract_fusion.4
  386.2 23.7 %custom-call.40 = f32[2,128,128]{2,1,0:T(8,128)S(1)} custom-call(f32[2,128,128]{2,1,0:T(8,128)S(1)} %convolution_subtract_fusion.4), custom_call_target="Cholesky" | custom-call | tf_op jit(solution)/shard_map/jit(cholesky)/cholesky | solution.py:20
  409.9 0.8 select_reduce_fusion.2
  410.6 0.1 compare_reduce_fusion.2
  410.8 0.2 compare_reduce_fusion
  411.0 2.8 select_select_fusion
  413.7 14.4 %while.1 = (s32[]{:T(128)}, f32[2,512,512]{2,1,0:T(8,128)}, s32[4,2]{0,1:T(2,128)S(1)}, f32[4,2,128,128]{3,2,0,1:T(8,128)}, s32[]{:T(128)}) while((s32[]{:T(128)}, f32[2,512,512]{2,1,0:T(8,128)}, s32[4,2]{0,1:T(2,128)S(1)}, f32[4,2,128,128]{3,2,0,1:T(8,128)}, s32[]{:T(128)}) %tuple.32), condition=%wide.while_cond, body=%wide.while_body.sunk | while | flops 2 | bytes 263777 | solution.py:21
  413.7 0.1 constant_dynamic-slice_fusion.2
  413.8 0.5 fusion.50
  414.3 3.0 bitcast_dynamic-update-slice_fusion.2
  417.4 0.1 constant_dynamic-slice_fusion.2
  417.4 0.5 fusion.50
  417.9 3.0 bitcast_dynamic-update-slice_fusion.2
  421.0 0.1 constant_dynamic-slice_fusion.2
  421.0 0.5 fusion.50
  421.6 3.0 bitcast_dynamic-update-slice_fusion.2
  424.6 0.1 constant_dynamic-slice_fusion.2
  424.7 0.5 fusion.50
  425.2 3.0 bitcast_dynamic-update-slice_fusion.2
  428.2 79.5 %custom-call.41 = f32[2,4,128,128]{2,3,1,0:T(8,128)S(1)} custom-call(f32[2,4,128,128]{3,2,1,0:T(8,128)} %bitcast.62), custom_call_target="InvertDiagBlocksLowerTriangular" | custom-call | tf_op jit(solution)/shard_map/triangular_solve | solution.py:21
  507.6 0.4 fusion.23
  508.0 1.3 convolution_subtract_fusion.5
  509.3 0.4 fusion.21
  509.7 1.6 convolution_subtract_fusion.3
  511.3 0.4 fusion.20
  511.7 1.8 convolution_subtract_fusion.2
  513.5 0.4 fusion.19
  513.9 1.7 fusion.30
  515.6 145.4 %all-reduce.9.cloned.1.call-done = f32[2,192,512]{2,1,0:T(8,128)} async-done(((f32[2,192,512]{2,1,0:T(8,128)}), f32[2,192,512]{2,1,0:T(8,128)}) %all-reduce.9.cloned.1.call-update) | async-done | bytes 786448 | tf_op jit(solution)/shard_map/psum | solution.py:25
  661.0 1.3 multiply_reduce_fusion
  662.3 17.1 %psum.31 = f32[2,512]{1,0:T(2,128)S(1)} all-reduce(f32[2,512]{1,0:T(2,128)S(1)} %multiply_reduce_fusion), channel_id=1, replica_groups=mesh['fsdp'=32,'tensor'=8] {'tensor'}, use_global_device_ids=true, to_apply=%region_12.13 | all-reduce | flops 1024 | bytes 8192 | tf_op jit(solution)/shard_map/psum | solution.py:26
  679.4 1.2 broadcast_multiply_fusion
  680.7 1.5 fusion.2
  682.2 1.5 fusion.1
  (26 shorter events, 0.2 us)
Async XLA Ops:
  7.2 1.1 copy-start
  7.2 71.3 %all-reduce.5.cloned.1.call-start = ((), (), s32[]{:S(2)}) async-start(), calls=%async_computation | async-start | bytes 1048576 | tf_op jit(solution)/shard_map/psum | solution.py:17
  10.8 223.3 %all-reduce.7.cloned.1.call-start = ((), (), s32[]{:S(2)}) async-start(), calls=%async_computation.1 | async-start | bytes 4194304 | tf_op jit(solution)/shard_map/psum | solution.py:19
  82.8 578.2 %all-reduce.9.cloned.1.call-start = ((), (), s32[]{:S(2)}) async-start(), calls=%async_computation.2 | async-start | bytes 1572864 | tf_op jit(solution)/shard_map/psum | solution.py:25
  234.1 3.0 copy-start.1
  239.2 1.4 copy-start.3
  410.9 2.8 copy-start.8
  411.0 96.7 %copy-start.4 = (f32[2,128,512]{2,1,0:T(8,128)S(1)}, f32[2,128,512]{2,1,0:T(8,128)}, u32[]{:S(2)}) copy-start(f32[2,128,512]{2,1,0:T(8,128)} %all-reduce.5.cloned.1.call-done) | copy-start | bytes 1572868
  428.2 85.8 %copy-start.6 = (f32[2,128,192]{1,2,0:T(8,128)S(1)}, f32[2,128,192]{1,2,0:T(8,128)}, u32[]{:S(2)}) copy-start(f32[2,128,192]{1,2,0:T(8,128)} %param.3) | copy-start | bytes 589828
  428.2 85.8 %copy-start.7 = (bf16[2,128,192]{1,2,0:T(8,128)(2,1)S(1)}, bf16[2,128,192]{1,2,0:T(8,128)(2,1)}, u32[]{:S(2)}) copy-start(bf16[2,128,192]{1,2,0:T(8,128)(2,1)} %param.4) | copy-start | bytes 294916
  661.0 21.1 %copy-start.2 = (f32[2,192,512]{2,1,0:T(8,128)S(1)}, f32[2,192,512]{2,1,0:T(8,128)}, u32[]{:S(2)}) copy-start(f32[2,192,512]{2,1,0:T(8,128)} %all-reduce.9.cloned.1.call-done) | copy-start | bytes 2359300
  680.7 3.0 copy-start.5
Sparse Core Ops, SparseCore 0:
  11.0 67.4 all-reduce.4
  83.0 151.1 all-reduce.6
  515.8 145.2 all-reduce.8
where the time goes:
time: 694 us; the launch traced here: 690 us
  waiting for transfers between devices  362 us (52%)
  other arithmetic  249 us (36%)
  matrix products  26.3 us (4%)
  local copies, waits for them, and re-layouts  21.5 us (3%)
  blocking collectives  17.1 us (2%)
  between operations  14.2 us (2%)
    another operation x16, other arithmetic, on_device(): factor = jnp.linalg.cholesky(gram)  161 us
    psum x1, waiting for transfers between devices, on_device(): gram = lax.psum(local_gram, 'fsdp')  149 us
    psum x1, waiting for transfers between devices, on_device(): coeffs = lax.psum(partial_coeffs, 'fsdp')  145 us
    another operation x4, other arithmetic, on_device(): lax.linalg.triangular_solve(factor, projected, left_side=False, lower=Tru...  83.6 us
    psum x1, waiting for transfers between devices, on_device(): projected = lax.psum(partial_proj, 'tensor')  67.6 us
    psum x1, blocking collectives, on_device(): squares = lax.psum(jnp.sum(coeffs * coeffs, axis=1), 'tensor')  17.1 us
    another operation x12, local copies, waits for them, and re-layouts  14.4 us
  transfers between devices with their start and end apart: 3, of which 3 were waited for; matrix products, arithmetic and copies ran while one was open for 0% of the time, Pallas kernels for 0%

commit v1 on v0

v1 whole, which is shorter than its diff:
```python
import functools
import math

import jax
import jax.numpy as jnp
from jax import lax
from jax.experimental import pallas as pl
from jax.experimental.pallas import tpu as pltpu
from jax.sharding import PartitionSpec as P

D = 4096
FF = 1536
RANK = 512
NX, NY, NZ = 4, 4, 8
ROWS = 128
COLS = 192
BLK = 128
NB = 16
F32 = jnp.float32
BF16 = jnp.bfloat16
HIGHEST = lax.Precision.HIGHEST
MESH = pl.DeviceIdType.MESH

PIECES = [
    [(s, c) for s in (x, 7 - x) for c in range(s // 2 + 1)] for x in range(NX)
]
PLACE = {piece: (x, n) for x in range(NX) for n, piece in enumerate(PIECES[x])}


def dot6(a, b, ca, cb):
    return lax.dot_general(
        a, b, (((ca,), (cb,)), ((), ())), precision=HIGHEST, preferred_element_type=F32
    )


def split(a):
    hi = a.astype(BF16)
    return hi, (a - hi.astype(F32)).astype(BF16)


def dot3(a, b, ca, cb):
    dims = (((ca,), (cb,)), ((), ()))
    ah, al = split(a)
    bh, bl = split(b)
    one = functools.partial(lax.dot_general, dimension_numbers=dims, preferred_element_type=F32)
    return one(ah, bh) + (one(ah, bl) + one(al, bh))


def invert_factor(m_ref, out_ref, vfull, pan, between):
    lane = lax.broadcasted_iota(jnp.int32, (NB, BLK), 1)
    sub = lax.broadcasted_iota(jnp.int32, (NB, BLK), 0)
    lane_all = lax.broadcasted_iota(jnp.int32, (BLK, BLK), 1)
    eye = lax.broadcasted_iota(jnp.int32, (BLK, BLK), 0) == lane_all
    diagonal = jnp.where(eye, m_ref[...], 0.0)
    scale_row = lax.rsqrt(jnp.sum(diagonal, axis=0, keepdims=True))
    scale_col = lax.rsqrt(jnp.sum(diagonal, axis=1, keepdims=True))
    scaled = m_ref[...] * scale_col * scale_row
    m_ref[...] = scaled
    pan[...] = scaled[:NB]
    vfull[...] = jnp.zeros_like(vfull)

    def columns(rows, rel):
        return [
            jnp.broadcast_to(
                jnp.sum(jnp.where(rel == j, rows, 0.0), axis=1, keepdims=True), (NB, BLK)
            )
            for j in range(NB)
        ]

    def step(b, carry):
        r0 = pl.multiple_of(b * NB, NB)
        before = pl.multiple_of(jnp.maximum(r0 - NB, 0), NB)
        after = pl.multiple_of(jnp.minimum(r0 + NB, BLK - NB), NB)
        rel = lane - r0
        inside = jnp.logical_and(rel >= 0, rel < NB)
        rel_all = lane_all - r0
        inside_before = jnp.logical_and(rel_all >= -NB, rel_all < 0)

        old = m_ref[...]
        m_ref[...] = jnp.where(inside_before, 0.0, old) - dot6(old, vfull[...], 1, 0)

        rows = pan[...]
        cols = jnp.stack(columns(rows, rel))
        full = jnp.where(inside, jnp.where(rel == sub, 1.0, 0.0), rows)
        lower = full
        scale = jnp.zeros((NB, BLK), F32)
        for p in range(0, NB, 2):
            u1, u2 = cols[0], cols[1]
            a, e, d = u1[p : p + 1], u2[p : p + 1], u2[p + 1 : p + 2]
            det = a * d - e * e
            inv = pl.reciprocal(det, approx=True)
            inv = inv * (2.0 - det * inv)
            v1, v2 = d * u1 - e * u2, a * u2 - e * u1
            ia = 1.0 / a
            under = sub > p + 1
            l1 = jnp.where(under, v1 * inv, jnp.where(sub == p + 1, e * ia, 0.0))
            l2 = jnp.where(under, v2 * inv, 0.0)
            lower = lower - (l1 * lower[p : p + 1] + l2 * lower[p + 1 : p + 2])
            scale = jnp.where(sub == p, lax.rsqrt(a), scale)
            scale = jnp.where(sub == p + 1, lax.rsqrt(det * ia), scale)
            v1 = jnp.where(sub == p, det - d, jnp.where(sub == p + 1, e, v1))
            v2 = jnp.where(sub == p, e, jnp.where(sub == p + 1, det - a, v2))
            full = full - (v1 * full[p : p + 1] + v2 * full[p + 1 : p + 2]) * inv
            if p + 2 < NB:
                rest = cols[2:]
                cols = rest - (v1[None] * rest[:, p : p + 1] + v2[None] * rest[:, p + 1 : p + 2]) * inv
        out_ref[pl.ds(r0, NB), :] = lower * scale * scale_row

        rows = m_ref[pl.ds(after, NB), :]
        terms = [m * full[j : j + 1] for j, m in enumerate(columns(rows, rel))]
        while len(terms) > 1:
            terms = [terms[i] + terms[i + 1] for i in range(0, len(terms), 2)]
        pan[...] = jnp.where(inside, 0.0, rows) - terms[0]
        vfull[pl.ds(before, NB), :] = jnp.zeros((NB, BLK), F32)
        vfull[pl.ds(r0, NB), :] = full
        return carry

    half = BLK // NB // 2
    lax.fori_loop(0, half, step, 0)
    between()
    lax.fori_loop(half, 2 * half, step, 0)


def kernel(
    mom_hbm, grad_hbm, basis_hbm, nm_hbm, nb_hbm, up_hbm,
    mom_ref, grad_ref, basis_ref, in_sem, b2, bsend, pown, poth, prcv, psum, pcomb, xrcv, pfull, gp, zrcv, gz, yrcv, gown, gfull,
    wp, wcomb, wyrcv, wy, wzrcv, wfull, afac, mblk, iblk, vfull, pan, qs, cs, sq, sqrcv, nms, nbs, ups, uprcv, nmo, nbo, upo, out_sem,
    s_pair, r_pair, s_xr, r_xr, s_xa, r_xa, s_zr, r_zr, s_y, r_y, s_gx, r_gx, s_gz, r_gz,
    s_wy, r_wy, s_wz, r_wz, s_wza, r_wza, s_wya, r_wya, s_n, r_n,
):
    f = lax.axis_index("fsdp")
    t = lax.axis_index("tensor")
    z, y = f // NY, f % NY
    x, c = t // 2, t % 2
    o = 1 - c

    pair = (f, x * 2 + o)

    def on_x(k):
        return (f, ((x + k + NX) % NX) * 2 + c)

    def on_y(k):
        return (z * NY + (y + k + NY) % NY, t)

    def on_z(k):
        return (((z + k) % NZ) * NY + y, t)

    s = 1 - 2 * c

    pending = []

    def send(src, dst, ssem, rsem, to):
        copy = pltpu.make_async_remote_copy(
            src_ref=src, dst_ref=dst, send_sem=ssem, recv_sem=rsem,
            device_id=to, device_id_type=MESH,
        )
        copy.start()
        pending.append(copy)
        return copy

    loads = [
        pltpu.make_async_copy(src, dst, in_sem.at[i])
        for i, (src, dst) in enumerate(
            (
                (mom_hbm, mom_ref),
                (grad_hbm, grad_ref),
                (basis_hbm.at[o], basis_ref.at[o]),
                (basis_hbm.at[c], basis_ref.at[c]),
            )
        )
    ]
    for load in loads:
        load.start()
    barrier = pltpu.get_barrier_semaphore()
    peers = [pair] + [on_x(k) for k in range(1, NX)]
    peers += [on_y(k) for k in range(1, NY)] + [on_z(k) for k in range(1, NZ)]
    for peer in peers:
        pl.semaphore_signal(barrier, inc=1, device_id=peer, device_id_type=MESH)

    for load in loads[:3]:
        load.wait()
    bsend[...] = mom_ref[o] + grad_ref[o].astype(F32)
    p = dot6(bsend[...], basis_ref[o], 0, 0)
    for b in range(4):
        poth[b] = p[:, b * BLK : (b + 1) * BLK]
    pl.semaphore_wait(barrier, len(peers))
    cp = send(poth, prcv, s_pair.at[0], r_pair.at[0], pair)
    cb = send(bsend, b2.at[c], s_pair.at[1], r_pair.at[1], pair)
    own = mom_ref[c] + grad_ref[c].astype(F32)
    b2[c] = own
    loads[3].wait()
    p = dot6(own, basis_ref[c], 0, 0)
    for b in range(4):
        pown[b] = p[:, b * BLK : (b + 1) * BLK]
    cp.wait_recv()
    for b in range(4):
        psum[b] = pown[b] + prcv[b]

    def sum_start(parts, me, own, own_sem, rcv, rcv_sem, to):
        far = send(parts.at[(me + 2) % 4], rcv.at[0], own_sem.at[0], rcv_sem.at[0], to(s))
        near = send(parts.at[(me - s + 4) % 4], rcv.at[1], own_sem.at[1], rcv_sem.at[1], to(-s))
        return far, near

    def sum_relay(started, parts, me, own, own_sem, rcv, rcv_sem, to):
        started[0].wait_recv()
        own[...] = parts[(me + s + 4) % 4] + rcv[0]
        return started[1], send(own, rcv.at[2], own_sem.at[2], rcv_sem.at[2], to(s))

    def sum_end(started, parts, me, own, own_sem, rcv, rcv_sem, to):
        for copy in started:
            copy.wait_recv()
        return parts[me] + rcv[1] + rcv[2]

    def gather_start(slot, me, ssem, rsem, to):
        return [send(slot(me), slot(me), ssem.at[i], rsem.at[i], to(k)) for i, k in enumerate((s, -s))]

    def gather_relay(started, slot, me, ssem, rsem, to):
        started[0].wait_recv()
        here = slot((me - s + 4) % 4)
        return [started[1], send(here, here, ssem.at[2], rsem.at[2], to(s))]

    args = (psum, x, pcomb, s_xr, xrcv, r_xr, on_x)
    pfull[x] = sum_end(sum_relay(sum_start(*args), *args), *args)
    args = (lambda i: pfull.at[i], x, s_xa, r_xa, on_x)
    for copy in gather_relay(gather_start(*args), *args):
        copy.wait_recv()

    for i in range(4):
        for j in range(i + 1):
            g = dot6(pfull[i], pfull[j], 0, 0)
            for h in range(2):
                at, n = PLACE[(2 * i + h, j)]
                gp[at, n] = g[h * 64 : (h + 1) * 64]

    def rows8(k):
        return pl.ds(pl.multiple_of(((z + k) % NZ) * 8, 8), 8)

    first, rest = pl.ds(0, 1), pl.ds(1, 4)
    around = (4, 3, 5, 2, 6, 1, 7)

    def gram_z(part, n):
        return [
            send(
                gp.at[x, n, rows8(k), :], zrcv.at[k - 1, n],
                s_zr.at[part, k - 1], r_zr.at[part, k - 1], on_z(k),
            )
            for k in around
        ]

    def gram_y(part, n, before):
        for copy in before:
            copy.wait_recv()
        total = gp[x, n, rows8(0), :]
        for k in range(NZ - 1):
            total = total + zrcv[k, n]
        gz[n] = total
        return [
            send(gz.at[n], yrcv.at[k - 1, n], s_y.at[part, k - 1], r_y.at[part, k - 1], on_y(k))
            for k in (2, 1, 3)
        ]

    def gram_gather_z(part, n, before):
        for copy in before:
            copy.wait_recv()
        total = gz[n]
        for k in range(NY - 1):
            total = total + yrcv[k, n]
        gown[n] = total
        gfull[x, n, rows8(0), :] = total
        return [
            send(
                gown.at[n], gfull.at[x, n, rows8(0), :],
                s_gz.at[part, k - 1], r_gz.at[part, k - 1], on_z(k),
            )
            for k in around
        ]

    w_rows = COLS * 2 // NZ

    def wrows(k):
        return pl.ds(pl.multiple_of(((z + k) % NZ) * w_rows, 8), w_rows)

    def w_sum_z(before):
        wy[...] = sum_end(before, *w_args)
        return [
            send(wy.at[wrows(k), :], wzrcv.at[k - 1], s_wz.at[k - 1], r_wz.at[k - 1], on_z(k))
            for k in around
        ]

    def w_gather_z(before):
        for copy in before:
            copy.wait_recv()
        total = wy[wrows(0), :]
        for k in range(NZ - 1):
            total = total + wzrcv[k]
        wfull[y, wrows(0), :] = total
        here = wfull.at[y, wrows(0), :]
        return [send(here, here, s_wza.at[k - 1], r_wza.at[k - 1], on_z(k)) for k in around]

    g0 = gram_z(0, first)
    g1 = gram_z(1, rest)
    cb.wait_recv()
    for i in range(2):
        for b in range(4):
            wp[b, i * COLS : (i + 1) * COLS, :] = dot6(b2[i], pfull[b], 1, 0)
    g0 = gram_y(0, first, g0)
    w_args = (wp, y, wcomb, s_wy, wyrcv, r_wy, on_y)
    w = sum_start(*w_args)
    g1 = gram_y(1, rest, g1)
    g0 = gram_gather_z(0, first, g0)
    g1 = gram_gather_z(1, rest, g1)
    w = sum_relay(w, *w_args)
    for copy in g0:
        copy.wait_recv()
    here = gfull.at[x, first]
    g0 = [send(here, here, s_gx.at[k + 2], r_gx.at[k + 2], on_x(k)) for k in (1, 3, 2)]
    for copy in g1:
        copy.wait_recv()
    g_args = (lambda i: gfull.at[i, rest], x, s_gx, r_gx, on_x)
    g1 = gather_start(*g_args)
    w = w_sum_z(w)
    for copy in g0:
        copy.wait_recv()

    wg_args = (lambda i: wfull.at[i], y, s_wya, r_wya, on_y)

    def w_gather_y(before):
        for copy in before:
            copy.wait_recv()
        return gather_start(*wg_args)

    def w_relay_y(before):
        return gather_relay(before, *wg_args)

    flights = {"w": w, "g": g1}

    def between(kb):
        if kb == 0:
            flights["g"] = gather_relay(flights["g"], *g_args)

    def after(kb):
        sent = list(pending)
        pending.clear()
        if kb == 0:
            flights["w"] = w_gather_z(flights["w"])
        if kb == 1:
            flights["w"] = w_gather_y(flights["w"])
        if kb == 2:
            flights["w"] = w_relay_y(flights["w"])
        for copy in sent:
            copy.wait_send()

    def load(i, j):
        return jnp.concatenate([gfull[PLACE[(2 * i + h, j)]] for h in range(2)], axis=0)

    def lanes(b):
        return slice(b * BLK, (b + 1) * BLK)

    tril = lax.broadcasted_iota(jnp.int32, (BLK, BLK), 0) >= lax.broadcasted_iota(
        jnp.int32, (BLK, BLK), 1
    )
    afac[0, 0] = load(0, 0)
    inverses = []
    for kb in range(4):
        mblk[...] = afac[kb, kb]
        invert_factor(mblk, iblk, vfull, pan, functools.partial(between, kb))
        inv = jnp.where(tril, iblk[...], 0.0)
        after(kb)
        if kb == 0:
            for copy in flights["g"]:
                copy.wait_recv()
            for i in range(1, 4):
                for j in range(i + 1):
                    afac[i, j] = load(i, j)
        for i in range(kb + 1, 4):
            afac[i, kb] = dot6(afac[i, kb], inv, 1, 1)
        for i in range(kb + 1, 4):
            for j in range(kb + 1, i + 1):
                afac[i, j] = afac[i, j] - dot6(afac[i, kb], afac[j, kb], 1, 1)
        q = pfull[kb]
        for j in range(kb):
            q = q - dot3(qs[:, lanes(j)], afac[kb, j], 1, 1)
        qs[:, lanes(kb)] = dot3(q, inv, 1, 1)
        inverses.append(inv)
    for copy in flights["w"]:
        copy.wait_recv()
    for kb in range(4):
        w = wfull[kb]
        for j in range(kb):
            w = w - dot3(cs[:, lanes(j)], afac[kb, j], 1, 1)
        cs[:, lanes(kb)] = dot3(w, inverses[kb], 1, 1)

    sq[...] = jnp.sum(cs[...] * cs[...], axis=0, keepdims=True)
    copies = [send(sq, sqrcv.at[k - 1], s_n.at[k - 1], r_n.at[k - 1], on_x(k)) for k in (2, 1, 3)]

    def half(i):
        return pl.ds(pl.multiple_of(i * COLS, 8), COLS)

    q16 = qs[...].astype(BF16)

    def error(i):
        return lax.dot_general(
            cs[half(i), :].astype(BF16), q16, (((1,), (1,)), ((), ())), preferred_element_type=F32
        )

    nms[...] = b2[o] - 0.05 * error(o)
    out_m = send(nms, nm_hbm.at[c], s_pair.at[2], r_pair.at[2], pair)
    nmo[...] = b2[c] - 0.05 * error(c)
    stores = [pltpu.make_async_copy(nmo, nm_hbm.at[c], out_sem.at[0])]
    stores[0].start()
    for copy in copies:
        copy.wait_recv()
    norm = lax.rsqrt(sq[...] + sqrcv[0] + sqrcv[1] + sqrcv[2] + 1e-06)
    nbs[...] = cs[half(o), :] * norm
    out_b = send(nbs, nb_hbm.at[c], s_pair.at[3], r_pair.at[3], pair)
    factor_scale = math.sqrt(D * FF / RANK)
    ups[...] = factor_scale * dot3(nbs[...], qs[...], 1, 1)
    out_u = send(ups, uprcv, s_pair.at[4], r_pair.at[4], pair)
    nbo[...] = cs[half(c), :] * norm
    stores.append(pltpu.make_async_copy(nbo, nb_hbm.at[c], out_sem.at[1]))
    stores[1].start()
    upo[c] = (factor_scale * dot3(nbo[...], qs[...], 1, 1)).astype(BF16)
    out_u.wait_recv()
    upo[o] = uprcv[...].astype(BF16)
    stores.append(pltpu.make_async_copy(upo, up_hbm, out_sem.at[2]))
    stores[2].start()
    out_m.wait_recv()
    out_b.wait_recv()
    for store in stores:
        store.wait()
    for copy in pending:
        copy.wait_send()


def finish(nm_from, nb_from, up_from, nm_to, nb_to, up_to, nm, nb, up, sem_in, sem_out):
    ins, outs = [], []
    refs = ((nb_from, nb, nb_to), (nm_from, nm, nm_to), (up_from, up, up_to))
    for i, (src, mid, dst) in enumerate(refs):
        for h in range(2):
            ins.append(pltpu.make_async_copy(src.at[h], mid.at[h], sem_in.at[i, h]))
            outs.append(pltpu.make_async_copy(mid.at[h], dst.at[h], sem_out.at[i, h]))
    for copy in ins:
        copy.start()
    for first, second in zip(ins, outs, strict=True):
        first.wait()
        second.start()
    for copy in outs:
        copy.wait()


def on_device(momentum, grad, basis):
    vm = pltpu.VMEM
    chunk = (4, BLK, BLK)
    w_rows = COLS * 2 // NZ
    scratch = [
        vm((2, COLS, ROWS), F32), vm((2, COLS, ROWS), BF16), vm((2, COLS, RANK), F32),
        pltpu.SemaphoreType.DMA((4,)),
        vm((2, COLS, ROWS), F32), vm((COLS, ROWS), F32),
        vm(chunk, F32), vm(chunk, F32), vm(chunk, F32), vm(chunk, F32),
        vm((BLK, BLK), F32), vm((3, BLK, BLK), F32), vm(chunk, F32),
        vm((4, 5, 64, BLK), F32), vm((7, 5, 8, BLK), F32), vm((5, 8, BLK), F32),
        vm((3, 5, 8, BLK), F32), vm((5, 8, BLK), F32), vm((4, 5, 64, BLK), F32),
        vm((4, 2 * COLS, BLK), F32), vm((2 * COLS, BLK), F32),
        vm((3, 2 * COLS, BLK), F32), vm((2 * COLS, BLK), F32),
        vm((7, w_rows, BLK), F32), vm((4, 2 * COLS, BLK), F32),
        vm((4, 4, BLK, BLK), F32), *[vm((BLK, BLK), F32)] * 3, vm((NB, BLK), F32),
        vm((ROWS, RANK), F32), vm((2 * COLS, RANK), F32),
        vm((1, RANK), F32), vm((3, 1, RANK), F32),
        vm((COLS, ROWS), F32), vm((COLS, RANK), F32), vm((COLS, ROWS), F32), vm((COLS, ROWS), F32),
        vm((COLS, ROWS), F32), vm((COLS, RANK), F32), vm((2, COLS, ROWS), BF16),
        pltpu.SemaphoreType.DMA((3,)),
    ]
    for n in (5, 3, 3, (2, 7), (2, 3), 6, (2, 7), 3, 7, 7, 3, 3):
        shape = n if isinstance(n, tuple) else (n,)
        scratch += [pltpu.SemaphoreType.DMA(shape), pltpu.SemaphoreType.DMA(shape)]
    hbm = pl.BlockSpec(memory_space=pl.ANY)
    shapes = (
        jax.ShapeDtypeStruct((2, COLS, ROWS), F32),
        jax.ShapeDtypeStruct((2, COLS, RANK), F32),
        jax.ShapeDtypeStruct((2, COLS, ROWS), BF16),
    )
    results = pl.pallas_call(
        kernel,
        out_shape=shapes,
        in_specs=[hbm] * 3,
        out_specs=(hbm,) * 3,
        scratch_shapes=scratch,
        compiler_params=pltpu.CompilerParams(
            collective_id=0, has_side_effects=True, vmem_limit_bytes=58 * 2**20
        ),
    )(jnp.swapaxes(momentum, 1, 2), jnp.swapaxes(grad, 1, 2), basis)
    nm, nb, up = pl.pallas_call(
        finish,
        out_shape=shapes,
        in_specs=[hbm] * 3,
        out_specs=(hbm,) * 3,
        scratch_shapes=[vm(shape.shape, shape.dtype) for shape in shapes]
        + [pltpu.SemaphoreType.DMA((3, 2))] * 2,
        compiler_params=pltpu.CompilerParams(vmem_limit_bytes=58 * 2**20),
    )(*results)
    return jnp.swapaxes(nm, 1, 2), nb, jnp.swapaxes(up, 1, 2)


def solution(mesh):
    in_specs = (P(None, "fsdp", "tensor"), P(None, "fsdp", "tensor"), P(None, "tensor", None))
    out_specs = (P(None, "fsdp", "tensor"), P(None, "tensor", None), P(None, "fsdp", "tensor"))
    return jax.shard_map(
        on_device, mesh=mesh, in_specs=in_specs, out_specs=out_specs, check_vma=False
    )
```

time: 694 us -> 78.4 us (0.11)
  waiting for transfers between devices: 362 us -> 0 us
  other arithmetic: 249 us -> 0 us
  Pallas kernels: 0 us -> 77.6 us
  matrix products: 26.3 us -> 0 us
  local copies, waits for them, and re-layouts: 21.5 us -> 0 us
  blocking collectives: 17.1 us -> 0 us
  between operations: 14.2 us -> 0.64 us
    psum x3 -> x0, waiting for transfers between devices: 362 us -> none  [the longest x1 149 us: on_device(): gram = lax.psum(local_gram, 'fsdp')]
    another operation x20 -> x0, other arithmetic: 244 us -> none  [the longest x16 161 us: on_device(): factor = jnp.linalg.cholesky(gram)]
    pallas_call x0 -> x2, Pallas kernels: none -> 77.6 us  [the longest x1 75.6 us: on_device(): pl.pallas_call(kernel, out_shape=shapes, in_specs=[hbm] * 3, out_specs=(h...]
    psum x1 -> x0, blocking collectives: 17.1 us -> none  [on_device(): squares = lax.psum(jnp.sum(coeffs * coeffs, axis=1), 'tensor')]
    another operation x17 -> x0, local copies, waits for them, and re-layouts: 16 us -> none
    another operation x13 -> x0, matrix products: 14.8 us -> none  [the longest x6 8.53 us: on_device(): factor = jnp.linalg.cholesky(gram)]
    dot_general x5 -> x0, matrix products: 11.5 us -> none  [the longest x1 4.32 us: on_device(): jnp.einsum('mdr,mds->mrs', projected, projected, precision=highest)]
  transfers between devices with their start and end apart: 3 -> 0, of which waited for: 3 -> 0; matrix products, arithmetic and copies ran while one was open for 0% -> 0% of each run, Pallas kernels for 0% -> 0%
where the time goes in v1:
time: 78.4 us; the launch traced here: 78.3 us
  Pallas kernels  77.6 us (99%)
    pallas_call x1, Pallas kernels, on_device(): pl.pallas_call(kernel, out_shape=shapes, in_specs=[hbm] * 3, out_specs=(h...  75.6 us
    pallas_call x1, Pallas kernels, on_device(): pl.pallas_call(finish, out_shape=shapes, in_specs=[hbm] * 3, out_specs=(h...  2.06 us

profile of v1, /device:TPU:1, one launch (start us, length us, event | category | flops | bytes accessed | tf_op | source)
XLA Modules:
  0.0 78.3 jit_solution(4966402259953443294)
XLA Ops:
  0.6 75.6 %shard_map.58 = (f32[2,192,128]{2,1,0:T(8,128)}, f32[2,192,512]{2,1,0:T(8,128)}, bf16[2,192,128]{2,1,0:T(8,128)(2,1)}) custom-call(f32[2,192,128]{2,1,0:T(8,128)} %bitcast.4, bf16[2,192,128]{2,1,0:T(8,128)(2,1)} %bitcast.5, f32[2,192,512]{2,1,0:T(8,128)} %basis_hbm.1), custom_call_target="tpu_custom_call" | custom-call | tf_op jit(solution)/shard_map/pallas_call | solution.py:482
  76.2 2.1 %shard_map.59 = (f32[2,192,128]{2,1,0:T(8,128)}, f32[2,192,512]{2,1,0:T(8,128)}, bf16[2,192,128]{2,1,0:T(8,128)(2,1)}) custom-call(f32[2,192,128]{2,1,0:T(8,128)} %get-tuple-element.9.nm_from, f32[2,192,512]{2,1,0:T(8,128)} %get-tuple-element.10.nb_from, bf16[2,192,128]{2,1,0:T(8,128)(2,1)} %get-tuple-element.11.up_from), custom_call_target="tpu_custom_call" | custom-call | tf_op jit(solution)/shard_map/pallas_call | solution.py:492

commit v2 on v1

v2 whole, which is shorter than its diff:
```python
import functools
import math

import jax
import jax.numpy as jnp
from jax import lax
from jax.experimental import pallas as pl
from jax.experimental.pallas import tpu as pltpu
from jax.sharding import PartitionSpec as P

D = 4096
FF = 1536
RANK = 512
NX, NY, NZ = 4, 4, 8
ROWS = 128
COLS = 192
BLK = 128
NB = 16
F32 = jnp.float32
BF16 = jnp.bfloat16
HIGHEST = lax.Precision.HIGHEST
MESH = pl.DeviceIdType.MESH

PLACE = {(2 * x + h, x): (x, h) for x in range(NX) for h in range(2)}
PLACE.update({(2 * (x + 1 - x // 3) + h, x % 3): (x, 2 + h) for x in range(NX) for h in range(2)})
PLACE.update({(2 * (2 + (x + 1) % 2) + x // 2, (x + 1) % 2): (x, 4) for x in range(NX)})


def dot6(a, b, ca, cb):
    return lax.dot_general(
        a, b, (((ca,), (cb,)), ((), ())), precision=HIGHEST, preferred_element_type=F32
    )


def split(a):
    hi = a.astype(BF16)
    return hi, (a - hi.astype(F32)).astype(BF16)


def dot3(a, b, ca, cb):
    dims = (((ca,), (cb,)), ((), ()))
    ah, al = split(a)
    bh, bl = split(b)
    one = functools.partial(lax.dot_general, dimension_numbers=dims, preferred_element_type=F32)
    return one(ah, bh) + (one(ah, bl) + one(al, bh))


def gram_long(a):
    hi = a.astype(BF16).astype(F32)
    rest = a - hi
    mid = rest.astype(BF16).astype(F32)
    low = rest - mid
    lhs = jnp.concatenate([hi, hi, hi, mid, mid, low], axis=0).astype(BF16)
    rhs = jnp.concatenate([hi, mid, low, hi, mid, hi], axis=0).astype(BF16)
    return lax.dot_general(lhs, rhs, (((0,), (0,)), ((), ())), preferred_element_type=F32)


def invert_factor(m_ref, out_ref, prev, pan, between):
    lane = lax.broadcasted_iota(jnp.int32, (NB, BLK), 1)
    sub = lax.broadcasted_iota(jnp.int32, (NB, BLK), 0)
    lane_all = lax.broadcasted_iota(jnp.int32, (BLK, BLK), 1)
    eye = lax.broadcasted_iota(jnp.int32, (BLK, BLK), 0) == lane_all
    diagonal = jnp.where(eye, m_ref[...], 0.0)
    scale_row = lax.rsqrt(jnp.sum(diagonal, axis=0, keepdims=True))
    scale_col = lax.rsqrt(jnp.sum(diagonal, axis=1, keepdims=True))
    scaled = m_ref[...] * scale_col * scale_row
    m_ref[...] = scaled
    pan[...] = scaled[:NB]
    prev[...] = jnp.zeros_like(prev)

    def columns(rows, rel):
        return [
            jnp.broadcast_to(
                jnp.sum(jnp.where(rel == j, rows, 0.0), axis=1, keepdims=True), (NB, BLK)
            )
            for j in range(NB)
        ]

    def step(b, carry):
        r0 = pl.multiple_of(b * NB, NB)
        after = pl.multiple_of(jnp.minimum(r0 + NB, BLK - NB), NB)
        rel = lane - r0
        inside = jnp.logical_and(rel >= 0, rel < NB)
        rel_all = lane_all - r0
        inside_before = jnp.logical_and(rel_all >= -NB, rel_all < 0)

        m_ref[...] = jnp.where(inside_before, 0.0, m_ref[...]) - gram_long(prev[...])

        rows = pan[...]
        cols = jnp.stack(columns(rows, rel))
        full = jnp.where(inside, jnp.where(rel == sub, 1.0, 0.0), rows)
        lower = full
        scale = jnp.zeros((NB, BLK), F32)
        for p in range(0, NB, 2):
            u1, u2 = cols[0], cols[1]
            a, e, d = u1[p : p + 1], u2[p : p + 1], u2[p + 1 : p + 2]
            det = a * d - e * e
            inv = pl.reciprocal(det, approx=True)
            inv = inv * (2.0 - det * inv)
            v1, v2 = d * u1 - e * u2, a * u2 - e * u1
            ia = 1.0 / a
            under = sub > p + 1
            l1 = jnp.where(under, v1 * inv, jnp.where(sub == p + 1, e * ia, 0.0))
            l2 = jnp.where(under, v2 * inv, 0.0)
            lower = lower - (l1 * lower[p : p + 1] + l2 * lower[p + 1 : p + 2])
            scale = jnp.where(sub == p, lax.rsqrt(a), scale)
            scale = jnp.where(sub == p + 1, lax.rsqrt(det * ia), scale)
            v1 = jnp.where(sub == p, det - d, jnp.where(sub == p + 1, e, v1))
            v2 = jnp.where(sub == p, e, jnp.where(sub == p + 1, det - a, v2))
            full = full - (v1 * full[p : p + 1] + v2 * full[p + 1 : p + 2]) * inv
            if p + 2 < NB:
                rest = cols[2:]
                cols = rest - (v1[None] * rest[:, p : p + 1] + v2[None] * rest[:, p + 1 : p + 2]) * inv
        lower = lower * scale
        prev[...] = lower
        out_ref[pl.ds(r0, NB), :] = lower * scale_row

        rows = m_ref[pl.ds(after, NB), :]
        terms = [m * full[j : j + 1] for j, m in enumerate(columns(rows, rel))]
        while len(terms) > 1:
            terms = [terms[i] + terms[i + 1] for i in range(0, len(terms), 2)]
        pan[...] = jnp.where(inside, 0.0, rows) - terms[0]
        return carry

    last = 0
    for b, call in between + [(BLK // NB, None)]:
        lax.fori_loop(last, b, step, 0)
        last = b
        if call is not None:
            call()


def kernel(
    mom_hbm, grad_hbm, basis_hbm, q_hbm, c_hbm, n_hbm,
    mom_ref, grad_ref, basis_ref, in_sem, b2, bsend, pown, poth, prcv, psum, pcomb, xrcv, pfull, halves, gp, zrcv, gz, yrcv, gown, gfull,
    wp, wcomb, wyrcv, wy, wzrcv, wfull, afac, mblk, iblk, prev, pan, qs, cs, sq, out_sem,
    s_pair, r_pair, s_xr, r_xr, s_xa, r_xa, s_zr, r_zr, s_y, r_y, s_gx, r_gx, s_gz, r_gz,
    s_wy, r_wy, s_wz, r_wz, s_wza, r_wza, s_wya, r_wya, s_end, r_end, s_n, r_n,
):
    f = lax.axis_index("fsdp")
    t = lax.axis_index("tensor")
    z, y = f // NY, f % NY
    x, c = t // 2, t % 2
    o = 1 - c

    pair = (f, x * 2 + o)

    def on_x(k):
        return (f, ((x + k + NX) % NX) * 2 + c)

    def on_y(k):
        return (z * NY + (y + k + NY) % NY, t)

    def on_z(k):
        return (((z + k) % NZ) * NY + y, t)

    s = 1 - 2 * c

    pending = []

    def make(src, dst, ssem, rsem, to):
        return pltpu.make_async_remote_copy(
            src_ref=src, dst_ref=dst, send_sem=ssem, recv_sem=rsem,
            device_id=to, device_id_type=MESH,
        )

    def send(*args):
        copy = make(*args)
        copy.start()
        pending.append(copy)
        return copy

    loads = [
        pltpu.make_async_copy(src, dst, in_sem.at[i])
        for i, (src, dst) in enumerate(
            (
                (mom_hbm, mom_ref),
                (grad_hbm, grad_ref),
                (basis_hbm.at[o], basis_ref.at[o]),
                (basis_hbm.at[c], basis_ref.at[c]),
            )
        )
    ]
    for load in loads:
        load.start()
    barrier = pltpu.get_barrier_semaphore()
    peers = [pair] + [on_x(k) for k in range(1, NX)]
    peers += [(f, ((x + k) % NX) * 2 + o) for k in range(1, NX)]
    peers += [on_y(k) for k in range(1, NY)] + [on_z(k) for k in range(1, NZ)]
    for peer in peers:
        pl.semaphore_signal(barrier, inc=1, device_id=peer, device_id_type=MESH)

    for load in loads[:3]:
        load.wait()
    bsend[...] = mom_ref[o] + grad_ref[o].astype(F32)
    p = dot3(bsend[...], basis_ref[o], 0, 0)
    for b in range(4):
        poth[b] = p[:, b * BLK : (b + 1) * BLK]
    pl.semaphore_wait(barrier, len(peers))
    cp = send(poth, prcv, s_pair.at[0], r_pair.at[0], pair)
    cb = send(bsend, b2.at[c], s_pair.at[1], r_pair.at[1], pair)
    own = mom_ref[c] + grad_ref[c].astype(F32)
    b2[c] = own
    loads[3].wait()
    p = dot3(own, basis_ref[c], 0, 0)
    for b in range(4):
        pown[b] = p[:, b * BLK : (b + 1) * BLK]
    cp.wait_recv()
    for b in range(4):
        psum[b] = pown[b] + prcv[b]

    def sum_start(parts, me, own, own_sem, rcv, rcv_sem, to):
        far = send(parts.at[(me + 2) % 4], rcv.at[0], own_sem.at[0], rcv_sem.at[0], to(s))
        near = send(parts.at[(me - s + 4) % 4], rcv.at[1], own_sem.at[1], rcv_sem.at[1], to(-s))
        return far, near

    def sum_relay(started, parts, me, own, own_sem, rcv, rcv_sem, to):
        started[0].wait_recv()
        own[...] = parts[(me + s + 4) % 4] + rcv[0]
        return started[1], send(own, rcv.at[2], own_sem.at[2], rcv_sem.at[2], to(s))

    def sum_end(started, parts, me, own, own_sem, rcv, rcv_sem, to):
        for copy in started:
            copy.wait_recv()
        return parts[me] + rcv[1] + rcv[2]

    def gather_start(slot, me, ssem, rsem, to):
        return [send(slot(me), slot(me), ssem.at[i], rsem.at[i], to(k)) for i, k in enumerate((s, -s))]

    def gather_relay(started, slot, me, ssem, rsem, to):
        here = slot((me - s + 4) % 4)
        return [started[1], send(here, here, ssem.at[2], rsem.at[2], to(s))]

    args = (psum, x, pcomb, s_xr, xrcv, r_xr, on_x)
    pfull[x] = sum_end(sum_relay(sum_start(*args), *args), *args)
    a_args = (lambda i: pfull.at[i], x, s_xa, r_xa, on_x)
    across = gather_start(*a_args)

    def rows8(k):
        return pl.ds(pl.multiple_of(((z + k) % NZ) * 8, 8), 8)

    first, rest = pl.ds(0, 2), pl.ds(2, 3)
    around = (4, 3, 5, 2, 6, 1, 7)

    def gram_z(part, n):
        return [
            send(
                gp.at[x, n, rows8(k), :], zrcv.at[k - 1, n],
                s_zr.at[part, k - 1], r_zr.at[part, k - 1], on_z(k),
            )
            for k in around
        ]

    def gram_y(part, n, before):
        for copy in before:
            copy.wait_recv()
        total = gp[x, n, rows8(0), :]
        for k in range(NZ - 1):
            total = total + zrcv[k, n]
        gz[n] = total
        return [
            send(gz.at[n], yrcv.at[k - 1, n], s_y.at[part, k - 1], r_y.at[part, k - 1], on_y(k))
            for k in (2, 1, 3)
        ]

    def gram_gather_z(part, n, before):
        for copy in before:
            copy.wait_recv()
        total = gz[n]
        for k in range(NY - 1):
            total = total + yrcv[k, n]
        gown[n] = total
        gfull[x, n, rows8(0), :] = total
        return [
            send(
                gown.at[n], gfull.at[x, n, rows8(0), :],
                s_gz.at[part, k - 1], r_gz.at[part, k - 1], on_z(k),
            )
            for k in around
        ]

    w_rows = COLS * 2 // NZ

    def wrows(k):
        return pl.ds(pl.multiple_of(((z + k) % NZ) * w_rows, 8), w_rows)

    def w_sum_z(before):
        wy[...] = sum_end(before, *w_args)
        return [
            send(wy.at[wrows(k), :], wzrcv.at[k - 1], s_wz.at[k - 1], r_wz.at[k - 1], on_z(k))
            for k in around
        ]

    def w_gather_z(before):
        for copy in before:
            copy.wait_recv()
        total = wy[wrows(0), :]
        for k in range(NZ - 1):
            total = total + wzrcv[k]
        wfull[y, wrows(0), :] = total
        here = wfull.at[y, wrows(0), :]
        return [send(here, here, s_wza.at[k - 1], r_wza.at[k - 1], on_z(k)) for k in around]

    g = dot6(pfull[x], pfull[x], 0, 0)
    for h in range(2):
        gp[x, h] = g[h * 64 : (h + 1) * 64]
    g0 = gram_z(0, first)
    across[0].wait_recv()
    far = gather_relay(across, *a_args)[1]
    across[1].wait_recv()
    g = dot6(pfull[x + 1 - x // 3], pfull[x % 3], 0, 0)
    for h in range(2):
        gp[x, 2 + h] = g[h * 64 : (h + 1) * 64]
    between_two = (x + 1) % 2
    g = dot6(pfull[between_two + 2], pfull[between_two], 0, 0)
    for h in range(2):
        halves[h] = g[h * 64 : (h + 1) * 64]
    gp[x, 4] = halves[x // 2]
    g1 = gram_z(1, rest)
    g0 = gram_y(0, first, g0)
    far.wait_recv()
    cb.wait_recv()
    for i in range(2):
        for b in range(4):
            wp[b, i * COLS : (i + 1) * COLS, :] = dot3(b2[i], pfull[b], 1, 0)
    g0 = gram_gather_z(0, first, g0)
    g1 = gram_y(1, rest, g1)
    w_args = (wp, y, wcomb, s_wy, wyrcv, r_wy, on_y)
    flights = {"w": sum_start(*w_args)}
    for copy in g0:
        copy.wait_recv()

    def diagonals():
        here = gfull.at[x, first]
        return [make(here, here, s_gx.at[k + 2], r_gx.at[k + 2], on_x(k)) for k in (1, 3, 2)]

    def diagonal_from(chip):
        k = (x - chip + NX) % NX
        here = gfull.at[chip, first]
        return make(here, here, s_gx.at[k + 2], r_gx.at[k + 2], on_x(k))

    @pl.when(x == 0)
    def _():
        for copy in diagonals():
            copy.start()

    flights["g"] = gram_gather_z(1, rest, g1)

    @pl.when(x != 0)
    def _():
        for copy in diagonals():
            copy.start()
        diagonal_from(0).wait_recv()

    g_args = (lambda i: gfull.at[i, rest], x, s_gx, r_gx, on_x)
    wg_args = (lambda i: wfull.at[i], y, s_wya, r_wya, on_y)

    def w_gather_y(before):
        for copy in before:
            copy.wait_recv()
        return gather_start(*wg_args)

    def w_relay():
        flights["w"] = sum_relay(flights["w"], *w_args)

    def w_to_z():
        flights["w"] = w_sum_z(flights["w"])

    def w_back_z():
        flights["w"] = w_gather_z(flights["w"])

    def w_back_y():
        flights["w"] = w_gather_y(flights["w"])

    def w_back_y_far():
        flights["w"][0].wait_recv()
        flights["w"] = gather_relay(flights["w"], *wg_args)

    def rest_near():
        for copy in flights["g"]:
            copy.wait_recv()
        flights["g"] = gather_start(*g_args)

    def rest_far():
        flights["g"][0].wait_recv()
        flights["g"] = gather_relay(flights["g"], *g_args)

    def rest_end():
        for chip in range(1, NX):

            @pl.when(x != chip)
            def _(chip=chip):
                diagonal_from(chip).wait_recv()

        for copy in flights["g"]:
            copy.wait_recv()

    def let_go():
        for copy in pending:
            copy.wait_send()
        pending.clear()

    between = [
        [(2, rest_near), (4, w_relay), (5, rest_far), (7, w_to_z)],
        [(4, w_back_z)],
        [(4, w_back_y)],
        [(4, w_back_y_far)],
    ]

    def load(i, j):
        return jnp.concatenate([gfull[PLACE[(2 * i + h, j)]] for h in range(2)], axis=0)

    def lanes(b):
        return slice(b * BLK, (b + 1) * BLK)

    def half(i):
        return pl.ds(pl.multiple_of(i * COLS, 8), COLS)

    tril = lax.broadcasted_iota(jnp.int32, (BLK, BLK), 0) >= lax.broadcasted_iota(
        jnp.int32, (BLK, BLK), 1
    )
    afac[0, 0] = load(0, 0)
    inverses = []
    for kb in range(4):
        mblk[...] = afac[kb, kb]
        invert_factor(mblk, iblk, prev, pan, between[kb])
        inv = jnp.where(tril, iblk[...], 0.0)
        if kb == 0:
            rest_end()
            for i in range(1, 4):
                for j in range(i + 1):
                    afac[i, j] = load(i, j)
        for i in range(kb + 1, 4):
            afac[i, kb] = dot6(afac[i, kb], inv, 1, 1)
        for i in range(kb + 1, 4):
            for j in range(kb + 1, i + 1):
                afac[i, j] = afac[i, j] - dot6(afac[i, kb], afac[j, kb], 1, 1)
        q = pfull[kb]
        for j in range(kb):
            q = q - dot3(qs[:, lanes(j)], afac[kb, j], 1, 1)
        qs[:, lanes(kb)] = dot3(q, inv, 1, 1)
        inverses.append(inv)
        if kb == 1:
            let_go()
    ends = [
        send(qs, q_hbm.at[c], s_end.at[0], r_end.at[0], pair),
        make(cs.at[half(o), :], c_hbm.at[c], s_end.at[1], r_end.at[1], pair),
    ]
    stores = [
        pltpu.make_async_copy(qs, q_hbm.at[c], out_sem.at[0]),
        pltpu.make_async_copy(cs.at[half(c), :], c_hbm.at[c], out_sem.at[1]),
        pltpu.make_async_copy(sq, n_hbm.at[c, x], out_sem.at[2]),
    ]
    stores[0].start()
    for copy in flights["w"]:
        copy.wait_recv()
    for kb in range(4):
        w = wfull[kb]
        for j in range(kb):
            w = w - dot3(cs[:, lanes(j)], afac[kb, j], 1, 1)
        cs[:, lanes(kb)] = dot3(w, inverses[kb], 1, 1)

    ends[1].start()
    stores[1].start()
    sq[...] = jnp.sum(cs[...] * cs[...], axis=0, keepdims=True)
    stores[2].start()
    sums = [
        send(sq, n_hbm.at[c, x], s_n.at[i], r_n.at[i], to)
        for i, to in enumerate(
            [on_x(2), on_x(1), on_x(3)]
            + [(f, ((x + k) % NX) * 2 + o) for k in (2, 1, 3, 0)]
        )
    ]
    for copy in pending[:-len(sums)]:
        copy.wait_send()
    for copy in diagonals():
        copy.wait_send()
    for copy in ends + sums:
        copy.wait_recv()
    ends[1].wait_send()
    for copy in sums:
        copy.wait_send()
    for store in stores:
        store.wait()


def finish(mom_ref, grad_ref, q_ref, c_ref, n_ref, nm_ref, nb_ref, up_ref):
    q, coeffs = q_ref[0], c_ref[0]
    error = lax.dot_general(
        coeffs.astype(BF16), q.astype(BF16), (((1,), (1,)), ((), ())), preferred_element_type=F32
    )
    nm_ref[0] = mom_ref[0] + grad_ref[0].astype(F32) - 0.05 * error
    basis = coeffs * lax.rsqrt(n_ref[0, 0] + n_ref[0, 1] + n_ref[0, 2] + n_ref[0, 3] + 1e-06)
    nb_ref[0] = basis
    up_ref[0] = (math.sqrt(D * FF / RANK) * dot3(basis, q, 1, 1)).astype(BF16)


def on_device(momentum, grad, basis):
    vm = pltpu.VMEM
    chunk = (4, BLK, BLK)
    w_rows = COLS * 2 // NZ
    scratch = [
        vm((2, COLS, ROWS), F32), vm((2, COLS, ROWS), BF16), vm((2, COLS, RANK), F32),
        pltpu.SemaphoreType.DMA((4,)),
        vm((2, COLS, ROWS), F32), vm((COLS, ROWS), F32),
        vm(chunk, F32), vm(chunk, F32), vm(chunk, F32), vm(chunk, F32),
        vm((BLK, BLK), F32), vm((3, BLK, BLK), F32), vm(chunk, F32),
        vm((2, 64, BLK), F32),
        vm((4, 5, 64, BLK), F32), vm((7, 5, 8, BLK), F32), vm((5, 8, BLK), F32),
        vm((3, 5, 8, BLK), F32), vm((5, 8, BLK), F32), vm((4, 5, 64, BLK), F32),
        vm((4, 2 * COLS, BLK), F32), vm((2 * COLS, BLK), F32),
        vm((3, 2 * COLS, BLK), F32), vm((2 * COLS, BLK), F32),
        vm((7, w_rows, BLK), F32), vm((4, 2 * COLS, BLK), F32),
        vm((4, 4, BLK, BLK), F32), *[vm((BLK, BLK), F32)] * 2, *[vm((NB, BLK), F32)] * 2,
        vm((ROWS, RANK), F32), vm((2 * COLS, RANK), F32),
        vm((1, RANK), F32),
        pltpu.SemaphoreType.DMA((3,)),
    ]
    for n in (2, 3, 3, (2, 7), (2, 3), 6, (2, 7), 3, 7, 7, 3, 2, 7):
        shape = n if isinstance(n, tuple) else (n,)
        scratch += [pltpu.SemaphoreType.DMA(shape), pltpu.SemaphoreType.DMA(shape)]
    hbm = pl.BlockSpec(memory_space=pl.ANY)
    momentum, grad = jnp.swapaxes(momentum, 1, 2), jnp.swapaxes(grad, 1, 2)
    q, coeffs, sums = pl.pallas_call(
        kernel,
        out_shape=(
            jax.ShapeDtypeStruct((2, ROWS, RANK), F32),
            jax.ShapeDtypeStruct((2, COLS, RANK), F32),
            jax.ShapeDtypeStruct((2, NX, 1, RANK), F32),
        ),
        in_specs=[hbm] * 3,
        out_specs=(hbm,) * 3,
        scratch_shapes=scratch,
        compiler_params=pltpu.CompilerParams(
            collective_id=0, has_side_effects=True, vmem_limit_bytes=58 * 2**20
        ),
    )(momentum, grad, basis)

    def one(*shape):
        return pl.BlockSpec((1, *shape), lambda i: (i,) + (0,) * len(shape))

    nm, nb, up = pl.pallas_call(
        finish,
        grid=(2,),
        out_shape=(
            jax.ShapeDtypeStruct((2, COLS, ROWS), F32),
            jax.ShapeDtypeStruct((2, COLS, RANK), F32),
            jax.ShapeDtypeStruct((2, COLS, ROWS), BF16),
        ),
        in_specs=[one(COLS, ROWS), one(COLS, ROWS), one(ROWS, RANK), one(COLS, RANK), one(NX, 1, RANK)],
        out_specs=(one(COLS, ROWS), one(COLS, RANK), one(COLS, ROWS)),
        compiler_params=pltpu.CompilerParams(vmem_limit_bytes=58 * 2**20),
    )(momentum, grad, q, coeffs, sums)
    return jnp.swapaxes(nm, 1, 2), nb, jnp.swapaxes(up, 1, 2)


def solution(mesh):
    in_specs = (P(None, "fsdp", "tensor"), P(None, "fsdp", "tensor"), P(None, "tensor", None))
    out_specs = (P(None, "fsdp", "tensor"), P(None, "tensor", None), P(None, "fsdp", "tensor"))
    return jax.shard_map(
        on_device, mesh=mesh, in_specs=in_specs, out_specs=out_specs, check_vma=False
    )
```

time: 78.4 us -> 74.4 us (0.949)
  Pallas kernels: 77.6 us -> 73.6 us
    pallas_call x2, Pallas kernels: 77.6 us -> 73.6 us  [the longest x1 71 us: on_device(): pl.pallas_call(kernel, out_shape=(jax.ShapeDtypeStruct((2, ROWS, RANK), F...]
where the time goes in v2:
time: 74.4 us; the launch traced here: 74.3 us
  Pallas kernels  73.6 us (99%)
    pallas_call x1, Pallas kernels, on_device(): pl.pallas_call(kernel, out_shape=(jax.ShapeDtypeStruct((2, ROWS, RANK), F...  71 us
    pallas_call x1, Pallas kernels, on_device(): pl.pallas_call(finish, grid=(2,), out_shape=(jax.ShapeDtypeStruct((2, COL...  2.61 us

profile of v2, /device:TPU:1, one launch (start us, length us, event | category | flops | bytes accessed | tf_op | source)
XLA Modules:
  0.0 74.3 jit_solution(11776605170367528008)
XLA Ops:
  0.6 71.0 %shard_map.58 = (f32[2,128,512]{2,1,0:T(8,128)}, f32[2,192,512]{2,1,0:T(8,128)}, f32[2,4,1,512]{3,2,1,0:T(1,128)}) custom-call(f32[2,192,128]{2,1,0:T(8,128)} %bitcast.4, bf16[2,192,128]{2,1,0:T(8,128)(2,1)} %bitcast.6, f32[2,192,512]{2,1,0:T(8,128)} %basis_hbm.1), custom_call_target="tpu_custom_call" | custom-call | tf_op jit(solution)/shard_map/pallas_call | solution.py:524
  71.6 2.6 %shard_map.59 = (f32[2,192,128]{2,1,0:T(8,128)}, f32[2,192,512]{2,1,0:T(8,128)}, bf16[2,192,128]{2,1,0:T(8,128)(2,1)}) custom-call(f32[2,192,128]{2,1,0:T(8,128)} %bitcast.5, bf16[2,192,128]{2,1,0:T(8,128)(2,1)} %bitcast.7, f32[2,128,512]{2,1,0:T(8,128)} %get-tuple-element.9.q_ref, f32[2,192,512]{2,1,0:T(8,128)} %get-tuple-element.10.c_ref, ...), custom_call_target="tpu_custom_call" | custom-call | tf_op jit(solution)/shard_map/pallas_call | solution.py:542

commit v3 on v2

--- a/solution.py
+++ b/solution.py
@@ -77,6 +77,8 @@
         ]
 
     def step(b, carry):
+        for at, call in between:
+            pl.when(b == at)(call)
         r0 = pl.multiple_of(b * NB, NB)
         after = pl.multiple_of(jnp.minimum(r0 + NB, BLK - NB), NB)
         rel = lane - r0
@@ -122,18 +124,13 @@
         pan[...] = jnp.where(inside, 0.0, rows) - terms[0]
         return carry
 
-    last = 0
-    for b, call in between + [(BLK // NB, None)]:
-        lax.fori_loop(last, b, step, 0)
-        last = b
-        if call is not None:
-            call()
+    lax.fori_loop(0, BLK // NB, step, 0)
 
 
 def kernel(
     mom_hbm, grad_hbm, basis_hbm, q_hbm, c_hbm, n_hbm,
     mom_ref, grad_ref, basis_ref, in_sem, b2, bsend, pown, poth, prcv, psum, pcomb, xrcv, pfull, halves, gp, zrcv, gz, yrcv, gown, gfull,
-    wp, wcomb, wyrcv, wy, wzrcv, wfull, afac, mblk, iblk, prev, pan, qs, cs, sq, out_sem,
+    wp, wcomb, wyrcv, wy, wzrcv, wfull, afac, xinv, mixed, mblk, iblk, prev, pan, qs, cs, sq, out_sem,
     s_pair, r_pair, s_xr, r_xr, s_xa, r_xa, s_zr, r_zr, s_y, r_y, s_gx, r_gx, s_gz, r_gz,
     s_wy, r_wy, s_wz, r_wz, s_wza, r_wza, s_wya, r_wya, s_end, r_end, s_n, r_n,
 ):
@@ -263,6 +260,12 @@
             for k in (2, 1, 3)
         ]
 
+    def gram_back_z(part, n):
+        here = gfull.at[x, n, rows8(0), :]
+        return [
+            make(gown.at[n], here, s_gz.at[part, k - 1], r_gz.at[part, k - 1], on_z(k)) for k in around
+        ]
+
     def gram_gather_z(part, n, before):
         for copy in before:
             copy.wait_recv()
@@ -271,35 +274,79 @@
             total = total + yrcv[k, n]
         gown[n] = total
         gfull[x, n, rows8(0), :] = total
+        copies = gram_back_z(part, n)
+        for copy in copies:
+            copy.start()
+        return copies
+
+    w_rows = COLS // NZ
+
+    def w_half(h):
+        return pl.ds(h * COLS, COLS)
+
+    def w_part(h, k):
+        return pl.ds(pl.multiple_of(h * COLS + ((z + k) % NZ) * w_rows, 8), w_rows)
+
+    def w_y(h):
+        rows = w_half(h)
+        return (
+            make(wp.at[(y + 2) % NY, rows, :], wyrcv.at[0, rows, :], s_wy.at[h, 0], r_wy.at[h, 0], on_y(s)),
+            make(wp.at[(y - s + NY) % NY, rows, :], wyrcv.at[1, rows, :], s_wy.at[h, 1], r_wy.at[h, 1], on_y(-s)),
+            make(wcomb.at[rows, :], wyrcv.at[2, rows, :], s_wy.at[h, 2], r_wy.at[h, 2], on_y(s)),
+        )
+
+    def w_z(h):
         return [
-            send(
-                gown.at[n], gfull.at[x, n, rows8(0), :],
-                s_gz.at[part, k - 1], r_gz.at[part, k - 1], on_z(k),
-            )
+            make(wy.at[w_part(h, k), :], wzrcv.at[h, k - 1], s_wz.at[h, k - 1], r_wz.at[h, k - 1], on_z(k))
             for k in around
         ]
 
-    w_rows = COLS * 2 // NZ
-
-    def wrows(k):
-        return pl.ds(pl.multiple_of(((z + k) % NZ) * w_rows, 8), w_rows)
-
-    def w_sum_z(before):
-        wy[...] = sum_end(before, *w_args)
-        return [
-            send(wy.at[wrows(k), :], wzrcv.at[k - 1], s_wz.at[k - 1], r_wz.at[k - 1], on_z(k))
-            for k in around
-        ]
-
-    def w_gather_z(before):
-        for copy in before:
-            copy.wait_recv()
-        total = wy[wrows(0), :]
-        for k in range(NZ - 1):
-            total = total + wzrcv[k]
-        wfull[y, wrows(0), :] = total
-        here = wfull.at[y, wrows(0), :]
-        return [send(here, here, s_wza.at[k - 1], r_wza.at[k - 1], on_z(k)) for k in around]
+    def w_back_z(h):
+        here = wfull.at[y, w_part(h, 0), :]
+        return [make(here, here, s_wza.at[h, k - 1], r_wza.at[h, k - 1], on_z(k)) for k in around]
+
+    def w_back_y(h):
+        here = wfull.at[y, w_half(h), :]
+        other = wfull.at[(y - s + NY) % NY, w_half(h), :]
+        return (
+            make(here, here, s_wya.at[h, 0], r_wya.at[h, 0], on_y(s)),
+            make(here, here, s_wya.at[h, 1], r_wya.at[h, 1], on_y(-s)),
+            make(other, other, s_wya.at[h, 2], r_wya.at[h, 2], on_y(s)),
+        )
+
+    def w_stage(stage, h):
+        rows = w_half(h)
+        if stage == 1:
+            _, _, relay = w_y(h)
+            w_y(h)[0].wait_recv()
+            wcomb[rows, :] = wp[(y + s + NY) % NY, rows, :] + wyrcv[0, rows, :]
+            relay.start()
+        if stage == 2:
+            for copy in w_y(h)[1:]:
+                copy.wait_recv()
+            wy[rows, :] = wp[y, rows, :] + wyrcv[1, rows, :] + wyrcv[2, rows, :]
+            for copy in w_z(h):
+                copy.start()
+        if stage == 3:
+            for copy in w_z(h):
+                copy.wait_recv()
+            total = wy[w_part(h, 0), :]
+            for k in range(NZ - 1):
+                total = total + wzrcv[h, k]
+            wfull[y, w_part(h, 0), :] = total
+            for copy in w_back_z(h):
+                copy.start()
+        if stage == 4:
+            for copy in w_back_z(h):
+                copy.wait_recv()
+            for copy in w_back_y(h)[:2]:
+                copy.start()
+        if stage == 5:
+            w_back_y(h)[0].wait_recv()
+            w_back_y(h)[2].start()
+        if stage == 6:
+            for copy in w_back_y(h)[1:]:
+                copy.wait_recv()
 
     g = dot6(pfull[x], pfull[x], 0, 0)
     for h in range(2):
@@ -320,13 +367,14 @@
     g0 = gram_y(0, first, g0)
     far.wait_recv()
     cb.wait_recv()
-    for i in range(2):
-        for b in range(4):
-            wp[b, i * COLS : (i + 1) * COLS, :] = dot3(b2[i], pfull[b], 1, 0)
+    for n, k in enumerate((2, NY - s, NY + s, 0)):
+        b = (y + k) % NY
+        for h in range(2):
+            wp[b, w_half(h), :] = dot3(b2[h], pfull[b], 1, 0)
+            if n < 2:
+                w_y(h)[n].start()
     g0 = gram_gather_z(0, first, g0)
     g1 = gram_y(1, rest, g1)
-    w_args = (wp, y, wcomb, s_wy, wyrcv, r_wy, on_y)
-    flights = {"w": sum_start(*w_args)}
     for copy in g0:
         copy.wait_recv()
 
@@ -344,7 +392,8 @@
         for copy in diagonals():
             copy.start()
 
-    flights["g"] = gram_gather_z(1, rest, g1)
+    gram_gather_z(1, rest, g1)
+    w_stage(1, 0)
 
     @pl.when(x != 0)
     def _():
@@ -352,38 +401,24 @@
             copy.start()
         diagonal_from(0).wait_recv()
 
-    g_args = (lambda i: gfull.at[i, rest], x, s_gx, r_gx, on_x)
-    wg_args = (lambda i: wfull.at[i], y, s_wya, r_wya, on_y)
-
-    def w_gather_y(before):
-        for copy in before:
+    def rest_x():
+        here = gfull.at[x, rest]
+        other = gfull.at[(x - s + NX) % NX, rest]
+        return (
+            make(here, here, s_gx.at[0], r_gx.at[0], on_x(s)),
+            make(here, here, s_gx.at[1], r_gx.at[1], on_x(-s)),
+            make(other, other, s_gx.at[2], r_gx.at[2], on_x(s)),
+        )
+
+    def rest_near():
+        for copy in gram_back_z(1, rest):
             copy.wait_recv()
-        return gather_start(*wg_args)
-
-    def w_relay():
-        flights["w"] = sum_relay(flights["w"], *w_args)
-
-    def w_to_z():
-        flights["w"] = w_sum_z(flights["w"])
-
-    def w_back_z():
-        flights["w"] = w_gather_z(flights["w"])
-
-    def w_back_y():
-        flights["w"] = w_gather_y(flights["w"])
-
-    def w_back_y_far():
-        flights["w"][0].wait_recv()
-        flights["w"] = gather_relay(flights["w"], *wg_args)
-
-    def rest_near():
-        for copy in flights["g"]:
-            copy.wait_recv()
-        flights["g"] = gather_start(*g_args)
+        for copy in rest_x()[:2]:
+            copy.start()
 
     def rest_far():
-        flights["g"][0].wait_recv()
-        flights["g"] = gather_relay(flights["g"], *g_args)
+        rest_x()[0].wait_recv()
+        rest_x()[2].start()
 
     def rest_end():
         for chip in range(1, NX):
@@ -392,7 +427,7 @@
             def _(chip=chip):
                 diagonal_from(chip).wait_recv()
 
-        for copy in flights["g"]:
+        for copy in rest_x()[1:]:
             copy.wait_recv()
 
     def let_go():
@@ -400,11 +435,14 @@
             copy.wait_send()
         pending.clear()
 
+    def stage(n, h):
+        return functools.partial(w_stage, n, h)
+
     between = [
-        [(2, rest_near), (4, w_relay), (5, rest_far), (7, w_to_z)],
-        [(4, w_back_z)],
-        [(4, w_back_y)],
-        [(4, w_back_y_far)],
+        [(2, stage(1, 1)), (2, rest_near), (5, rest_far), (6, stage(2, 0))],
+        [(3, stage(3, 0)), (7, stage(3, 1))],
+        [(4, stage(4, 0)), (7, stage(4, 1))],
+        [(2, stage(5, 0)), (6, stage(5, 1))],
     ]
 
     def load(i, j):
@@ -419,13 +457,18 @@
     tril = lax.broadcasted_iota(jnp.int32, (BLK, BLK), 0) >= lax.broadcasted_iota(
         jnp.int32, (BLK, BLK), 1
     )
+    def span(i, j):
+        return slice(i * BLK, j * BLK)
+
+    projected = jnp.concatenate([pfull[b] for b in range(4)], axis=1)
     afac[0, 0] = load(0, 0)
-    inverses = []
     for kb in range(4):
         mblk[...] = afac[kb, kb]
         invert_factor(mblk, iblk, prev, pan, between[kb])
         inv = jnp.where(tril, iblk[...], 0.0)
+        xinv[span(kb, kb + 1), span(kb, kb + 1)] = inv
         if kb == 0:
+            w_stage(2, 1)
             rest_end()
             for i in range(1, 4):
                 for j in range(i + 1):
@@ -435,11 +478,17 @@
         for i in range(kb + 1, 4):
             for j in range(kb + 1, i + 1):
                 afac[i, j] = afac[i, j] - dot6(afac[i, kb], afac[j, kb], 1, 1)
-        q = pfull[kb]
-        for j in range(kb):
-            q = q - dot3(qs[:, lanes(j)], afac[kb, j], 1, 1)
-        qs[:, lanes(kb)] = dot3(q, inv, 1, 1)
-        inverses.append(inv)
+        if kb > 0:
+            xinv[span(kb, kb + 1), span(0, kb)] = -dot3(inv, mixed[:, span(0, kb)], 1, 0)
+        qs[:, lanes(kb)] = dot3(
+            projected[:, span(0, kb + 1)], xinv[span(kb, kb + 1), span(0, kb + 1)], 1, 1
+        )
+        if kb < 3:
+            for j in range(kb + 1):
+                mixed[:, span(j, j + 1)] = sum(
+                    dot3(afac[kb + 1, i], xinv[span(i, i + 1), span(j, j + 1)], 1, 0)
+                    for i in range(j, kb + 1)
+                )
         if kb == 1:
             let_go()
     ends = [
@@ -452,14 +501,14 @@
         pltpu.make_async_copy(sq, n_hbm.at[c, x], out_sem.at[2]),
     ]
     stores[0].start()
-    for copy in flights["w"]:
-        copy.wait_recv()
-    for kb in range(4):
-        w = wfull[kb]
-        for j in range(kb):
-            w = w - dot3(cs[:, lanes(j)], afac[kb, j], 1, 1)
-        cs[:, lanes(kb)] = dot3(w, inverses[kb], 1, 1)
-
+    for h in range(2):
+        w_stage(6, h)
+        rows = w_half(h)
+        w = jnp.concatenate([wfull[b, rows, :] for b in range(4)], axis=1)
+        for kb in range(4):
+            cs[rows, lanes(kb)] = dot3(
+                w[:, span(0, kb + 1)], xinv[span(kb, kb + 1), span(0, kb + 1)], 1, 1
+            )
     ends[1].start()
     stores[1].start()
     sq[...] = jnp.sum(cs[...] * cs[...], axis=0, keepdims=True)
@@ -473,8 +522,11 @@
     ]
     for copy in pending[:-len(sums)]:
         copy.wait_send()
-    for copy in diagonals():
+    for copy in diagonals() + list(rest_x()) + gram_back_z(0, first) + gram_back_z(1, rest):
         copy.wait_send()
+    for h in range(2):
+        for copy in list(w_y(h)) + w_z(h) + w_back_z(h) + list(w_back_y(h)):
+            copy.wait_send()
     for copy in ends + sums:
         copy.wait_recv()
     ends[1].wait_send()
@@ -498,7 +550,6 @@
 def on_device(momentum, grad, basis):
     vm = pltpu.VMEM
     chunk = (4, BLK, BLK)
-    w_rows = COLS * 2 // NZ
     scratch = [
         vm((2, COLS, ROWS), F32), vm((2, COLS, ROWS), BF16), vm((2, COLS, RANK), F32),
         pltpu.SemaphoreType.DMA((4,)),
@@ -510,13 +561,14 @@
         vm((3, 5, 8, BLK), F32), vm((5, 8, BLK), F32), vm((4, 5, 64, BLK), F32),
         vm((4, 2 * COLS, BLK), F32), vm((2 * COLS, BLK), F32),
         vm((3, 2 * COLS, BLK), F32), vm((2 * COLS, BLK), F32),
-        vm((7, w_rows, BLK), F32), vm((4, 2 * COLS, BLK), F32),
-        vm((4, 4, BLK, BLK), F32), *[vm((BLK, BLK), F32)] * 2, *[vm((NB, BLK), F32)] * 2,
+        vm((2, 7, COLS // NZ, BLK), F32), vm((4, 2 * COLS, BLK), F32),
+        vm((4, 4, BLK, BLK), F32), vm((RANK, RANK), F32), vm((BLK, RANK), F32),
+        *[vm((BLK, BLK), F32)] * 2, *[vm((NB, BLK), F32)] * 2,
         vm((ROWS, RANK), F32), vm((2 * COLS, RANK), F32),
         vm((1, RANK), F32),
         pltpu.SemaphoreType.DMA((3,)),
     ]
-    for n in (2, 3, 3, (2, 7), (2, 3), 6, (2, 7), 3, 7, 7, 3, 2, 7):
+    for n in (2, 3, 3, (2, 7), (2, 3), 6, (2, 7), (2, 3), (2, 7), (2, 7), (2, 3), 2, 7):
         shape = n if isinstance(n, tuple) else (n,)
         scratch += [pltpu.SemaphoreType.DMA(shape), pltpu.SemaphoreType.DMA(shape)]
     hbm = pl.BlockSpec(memory_space=pl.ANY)

time: 74.4 us -> 70.7 us (0.950)
  Pallas kernels: 73.6 us -> 69.9 us
    pallas_call x1, Pallas kernels: 71 us -> 67.3 us  [on_device(): pl.pallas_call(kernel, out_shape=(jax.ShapeDtypeStruct((2, ROWS, RANK), F...]
where the time goes in v3:
time: 70.7 us; the launch traced here: 70.5 us
  Pallas kernels  69.9 us (99%)
    pallas_call x1, Pallas kernels, on_device(): pl.pallas_call(kernel, out_shape=(jax.ShapeDtypeStruct((2, ROWS, RANK), F...  67.3 us
    pallas_call x1, Pallas kernels, on_device(): pl.pallas_call(finish, grid=(2,), out_shape=(jax.ShapeDtypeStruct((2, COL...  2.61 us

profile of v3, /device:TPU:1, one launch (start us, length us, event | category | flops | bytes accessed | tf_op | source)
XLA Modules:
  0.0 70.5 jit_solution(1272316794444062814)
XLA Ops:
  0.6 67.3 %shard_map.58 = (f32[2,128,512]{2,1,0:T(8,128)}, f32[2,192,512]{2,1,0:T(8,128)}, f32[2,4,1,512]{3,2,1,0:T(1,128)}) custom-call(f32[2,192,128]{2,1,0:T(8,128)} %bitcast.4, bf16[2,192,128]{2,1,0:T(8,128)(2,1)} %bitcast.6, f32[2,192,512]{2,1,0:T(8,128)} %basis_hbm.1), custom_call_target="tpu_custom_call" | custom-call | tf_op jit(solution)/shard_map/pallas_call | solution.py:576
  67.9 2.6 %shard_map.59 = (f32[2,192,128]{2,1,0:T(8,128)}, f32[2,192,512]{2,1,0:T(8,128)}, bf16[2,192,128]{2,1,0:T(8,128)(2,1)}) custom-call(f32[2,192,128]{2,1,0:T(8,128)} %bitcast.5, bf16[2,192,128]{2,1,0:T(8,128)(2,1)} %bitcast.7, f32[2,128,512]{2,1,0:T(8,128)} %get-tuple-element.9.q_ref, f32[2,192,512]{2,1,0:T(8,128)} %get-tuple-element.10.c_ref, ...), custom_call_target="tpu_custom_call" | custom-call | tf_op jit(solution)/shard_map/pallas_call | solution.py:594

commit v4 on v3

--- a/solution.py
+++ b/solution.py
@@ -439,10 +439,10 @@
         return functools.partial(w_stage, n, h)
 
     between = [
-        [(2, stage(1, 1)), (2, rest_near), (5, rest_far), (6, stage(2, 0))],
-        [(3, stage(3, 0)), (7, stage(3, 1))],
-        [(4, stage(4, 0)), (7, stage(4, 1))],
-        [(2, stage(5, 0)), (6, stage(5, 1))],
+        [(1, stage(1, 1)), (2, rest_near), (4, stage(2, 0)), (5, rest_far), (7, stage(2, 1))],
+        [(1, stage(3, 0)), (4, stage(3, 1)), (7, stage(4, 0))],
+        [(1, stage(4, 1)), (4, stage(5, 0)), (7, stage(5, 1))],
+        [],
     ]
 
     def load(i, j):
@@ -468,7 +468,6 @@
         inv = jnp.where(tril, iblk[...], 0.0)
         xinv[span(kb, kb + 1), span(kb, kb + 1)] = inv
         if kb == 0:
-            w_stage(2, 1)
             rest_end()
             for i in range(1, 4):
                 for j in range(i + 1):

time: 70.7 us -> 71.3 us (level)
  no operation moved by 1% of the time
where the time goes in v4:
time: 71.3 us; the launch traced here: 71.2 us
  Pallas kernels  70.5 us (99%)
    pallas_call x1, Pallas kernels, on_device(): pl.pallas_call(kernel, out_shape=(jax.ShapeDtypeStruct((2, ROWS, RANK), F...  67.9 us
    pallas_call x1, Pallas kernels, on_device(): pl.pallas_call(finish, grid=(2,), out_shape=(jax.ShapeDtypeStruct((2, COL...  2.61 us

profile of v4, /device:TPU:1, one launch (start us, length us, event | category | flops | bytes accessed | tf_op | source)
XLA Modules:
  0.0 71.2 jit_solution(15801013695208540672)
XLA Ops:
  0.6 67.9 %shard_map.58 = (f32[2,128,512]{2,1,0:T(8,128)}, f32[2,192,512]{2,1,0:T(8,128)}, f32[2,4,1,512]{3,2,1,0:T(1,128)}) custom-call(f32[2,192,128]{2,1,0:T(8,128)} %bitcast.4, bf16[2,192,128]{2,1,0:T(8,128)(2,1)} %bitcast.6, f32[2,192,512]{2,1,0:T(8,128)} %basis_hbm.1), custom_call_target="tpu_custom_call" | custom-call | tf_op jit(solution)/shard_map/pallas_call | solution.py:575
  68.6 2.6 %shard_map.59 = (f32[2,192,128]{2,1,0:T(8,128)}, f32[2,192,512]{2,1,0:T(8,128)}, bf16[2,192,128]{2,1,0:T(8,128)(2,1)}) custom-call(f32[2,192,128]{2,1,0:T(8,128)} %bitcast.5, bf16[2,192,128]{2,1,0:T(8,128)(2,1)} %bitcast.7, f32[2,128,512]{2,1,0:T(8,128)} %get-tuple-element.9.q_ref, f32[2,192,512]{2,1,0:T(8,128)} %get-tuple-element.10.c_ref, ...), custom_call_target="tpu_custom_call" | custom-call | tf_op jit(solution)/shard_map/pallas_call | solution.py:593

commit v5 on v3

--- a/solution.py
+++ b/solution.py
@@ -102,17 +102,18 @@
             v1, v2 = d * u1 - e * u2, a * u2 - e * u1
             ia = 1.0 / a
             under = sub > p + 1
-            l1 = jnp.where(under, v1 * inv, jnp.where(sub == p + 1, e * ia, 0.0))
-            l2 = jnp.where(under, v2 * inv, 0.0)
+            w1, w2 = v1 * inv, v2 * inv
+            l1 = jnp.where(under, w1, jnp.where(sub == p + 1, e * ia, 0.0))
+            l2 = jnp.where(under, w2, 0.0)
             lower = lower - (l1 * lower[p : p + 1] + l2 * lower[p + 1 : p + 2])
             scale = jnp.where(sub == p, lax.rsqrt(a), scale)
             scale = jnp.where(sub == p + 1, lax.rsqrt(det * ia), scale)
-            v1 = jnp.where(sub == p, det - d, jnp.where(sub == p + 1, e, v1))
-            v2 = jnp.where(sub == p, e, jnp.where(sub == p + 1, det - a, v2))
-            full = full - (v1 * full[p : p + 1] + v2 * full[p + 1 : p + 2]) * inv
+            w1 = jnp.where(sub == p, 1.0 - d * inv, jnp.where(sub == p + 1, e * inv, w1))
+            w2 = jnp.where(sub == p, e * inv, jnp.where(sub == p + 1, 1.0 - a * inv, w2))
             if p + 2 < NB:
                 rest = cols[2:]
-                cols = rest - (v1[None] * rest[:, p : p + 1] + v2[None] * rest[:, p + 1 : p + 2]) * inv
+                cols = rest - (w1[None] * rest[:, p : p + 1] + w2[None] * rest[:, p + 1 : p + 2])
+            full = full - (w1 * full[p : p + 1] + w2 * full[p + 1 : p + 2])
         lower = lower * scale
         prev[...] = lower
         out_ref[pl.ds(r0, NB), :] = lower * scale_row
@@ -460,37 +461,51 @@
     def span(i, j):
         return slice(i * BLK, j * BLK)
 
-    projected = jnp.concatenate([pfull[b] for b in range(4)], axis=1)
-    afac[0, 0] = load(0, 0)
+    xinv[...] = jnp.zeros_like(xinv)
+    mblk[...] = load(0, 0)
     for kb in range(4):
-        mblk[...] = afac[kb, kb]
+        here, below, done = span(kb, kb + 1), span(kb + 1, 4), span(0, kb + 1)
         invert_factor(mblk, iblk, prev, pan, between[kb])
         inv = jnp.where(tril, iblk[...], 0.0)
-        xinv[span(kb, kb + 1), span(kb, kb + 1)] = inv
+        xinv[here, here] = inv
         if kb == 0:
             w_stage(2, 1)
             rest_end()
             for i in range(1, 4):
                 for j in range(i + 1):
-                    afac[i, j] = load(i, j)
-        for i in range(kb + 1, 4):
-            afac[i, kb] = dot6(afac[i, kb], inv, 1, 1)
-        for i in range(kb + 1, 4):
-            for j in range(kb + 1, i + 1):
-                afac[i, j] = afac[i, j] - dot6(afac[i, kb], afac[j, kb], 1, 1)
+                    afac[span(i, i + 1), span(j, j + 1)] = load(i, j)
+        if kb < 3:
+            panel = dot6(afac[below, here], inv, 1, 1)
+            afac[below, here] = panel
+            mblk[...] = afac[span(kb + 1, kb + 2), span(kb + 1, kb + 2)] - dot6(
+                panel[:BLK], panel[:BLK], 1, 1
+            )
+            for j in range(kb + 1, 3):
+                under, column = span(j + 1, 4), span(j, j + 1)
+                at = (j - kb - 1) * BLK
+                afac[under, column] = afac[under, column] - dot6(
+                    panel[at + BLK :], panel[at : at + BLK], 1, 1
+                )
+                corner = span(j + 1, j + 2)
+                afac[corner, corner] = afac[corner, corner] - dot6(
+                    panel[at + BLK : at + 2 * BLK], panel[at + BLK : at + 2 * BLK], 1, 1
+                )
         if kb > 0:
-            xinv[span(kb, kb + 1), span(0, kb)] = -dot3(inv, mixed[:, span(0, kb)], 1, 0)
-        qs[:, lanes(kb)] = dot3(
-            projected[:, span(0, kb + 1)], xinv[span(kb, kb + 1), span(0, kb + 1)], 1, 1
-        )
+            xinv[here, span(0, kb)] = -dot3(inv, mixed[:, span(0, kb)], 1, 0)
         if kb < 3:
-            for j in range(kb + 1):
-                mixed[:, span(j, j + 1)] = sum(
-                    dot3(afac[kb + 1, i], xinv[span(i, i + 1), span(j, j + 1)], 1, 0)
-                    for i in range(j, kb + 1)
-                )
+            mixed[:, done] = dot3(afac[span(kb + 1, kb + 2), done], xinv[done, done], 1, 0)
         if kb == 1:
             let_go()
+    for h in range(2):
+        w_stage(6, h)
+    both = jnp.concatenate(
+        [jnp.concatenate([pfull[b], wfull[b]], axis=0) for b in range(4)], axis=1
+    )
+    for kb in range(4):
+        done = span(0, kb + 1)
+        result = dot3(both[:, done], xinv[span(kb, kb + 1), done], 1, 1)
+        qs[:, lanes(kb)] = result[:ROWS]
+        cs[:, lanes(kb)] = result[ROWS:]
     ends = [
         send(qs, q_hbm.at[c], s_end.at[0], r_end.at[0], pair),
         make(cs.at[half(o), :], c_hbm.at[c], s_end.at[1], r_end.at[1], pair),
@@ -501,14 +516,6 @@
         pltpu.make_async_copy(sq, n_hbm.at[c, x], out_sem.at[2]),
     ]
     stores[0].start()
-    for h in range(2):
-        w_stage(6, h)
-        rows = w_half(h)
-        w = jnp.concatenate([wfull[b, rows, :] for b in range(4)], axis=1)
-        for kb in range(4):
-            cs[rows, lanes(kb)] = dot3(
-                w[:, span(0, kb + 1)], xinv[span(kb, kb + 1), span(0, kb + 1)], 1, 1
-            )
     ends[1].start()
     stores[1].start()
     sq[...] = jnp.sum(cs[...] * cs[...], axis=0, keepdims=True)
@@ -562,7 +569,7 @@
         vm((4, 2 * COLS, BLK), F32), vm((2 * COLS, BLK), F32),
         vm((3, 2 * COLS, BLK), F32), vm((2 * COLS, BLK), F32),
         vm((2, 7, COLS // NZ, BLK), F32), vm((4, 2 * COLS, BLK), F32),
-        vm((4, 4, BLK, BLK), F32), vm((RANK, RANK), F32), vm((BLK, RANK), F32),
+        vm((RANK, RANK), F32), vm((RANK, RANK), F32), vm((BLK, RANK), F32),
         *[vm((BLK, BLK), F32)] * 2, *[vm((NB, BLK), F32)] * 2,
         vm((ROWS, RANK), F32), vm((2 * COLS, RANK), F32),
         vm((1, RANK), F32),

time: 70.7 us -> 71.1 us (level)
  no operation moved by 1% of the time
where the time goes in v5:
time: 71.1 us; the launch traced here: 71 us
  Pallas kernels  70.4 us (99%)
    pallas_call x1, Pallas kernels, on_device(): pl.pallas_call(kernel, out_shape=(jax.ShapeDtypeStruct((2, ROWS, RANK), F...  67.8 us
    pallas_call x1, Pallas kernels, on_device(): pl.pallas_call(finish, grid=(2,), out_shape=(jax.ShapeDtypeStruct((2, COL...  2.61 us

profile of v5, /device:TPU:1, one launch (start us, length us, event | category | flops | bytes accessed | tf_op | source)
XLA Modules:
  0.0 71.0 jit_solution(16758246197212082016)
XLA Ops:
  0.6 67.8 %shard_map.58 = (f32[2,128,512]{2,1,0:T(8,128)}, f32[2,192,512]{2,1,0:T(8,128)}, f32[2,4,1,512]{3,2,1,0:T(1,128)}) custom-call(f32[2,192,128]{2,1,0:T(8,128)} %bitcast.4, bf16[2,192,128]{2,1,0:T(8,128)(2,1)} %bitcast.6, f32[2,192,512]{2,1,0:T(8,128)} %basis_hbm.1), custom_call_target="tpu_custom_call" | custom-call | tf_op jit(solution)/shard_map/pallas_call | solution.py:583
  68.4 2.6 %shard_map.59 = (f32[2,192,128]{2,1,0:T(8,128)}, f32[2,192,512]{2,1,0:T(8,128)}, bf16[2,192,128]{2,1,0:T(8,128)(2,1)}) custom-call(f32[2,192,128]{2,1,0:T(8,128)} %bitcast.5, bf16[2,192,128]{2,1,0:T(8,128)(2,1)} %bitcast.7, f32[2,128,512]{2,1,0:T(8,128)} %get-tuple-element.9.q_ref, f32[2,192,512]{2,1,0:T(8,128)} %get-tuple-element.10.c_ref, ...), custom_call_target="tpu_custom_call" | custom-call | tf_op jit(solution)/shard_map/pallas_call | solution.py:601

commit v6 on v5

--- a/solution.py
+++ b/solution.py
@@ -130,8 +130,8 @@
 
 def kernel(
     mom_hbm, grad_hbm, basis_hbm, q_hbm, c_hbm, n_hbm,
-    mom_ref, grad_ref, basis_ref, in_sem, b2, bsend, pown, poth, prcv, psum, pcomb, xrcv, pfull, halves, gp, zrcv, gz, yrcv, gown, gfull,
-    wp, wcomb, wyrcv, wy, wzrcv, wfull, afac, xinv, mixed, mblk, iblk, prev, pan, qs, cs, sq, out_sem,
+    mom_ref, grad_ref, basis_ref, in_sem, b2, bsend, pown, poth, prcv, psum, pcomb, xrcv, pfull, halves, gp, zrcv, gz, yrcv, gown, gfull, g10,
+    wp, wyrcv, wy, wzrcv, wfull, afac, xinv, mixed, mblk, iblk, prev, pan, qs, cs, sq, out_sem,
     s_pair, r_pair, s_xr, r_xr, s_xa, r_xa, s_zr, r_zr, s_y, r_y, s_gx, r_gx, s_gz, r_gz,
     s_wy, r_wy, s_wz, r_wz, s_wza, r_wza, s_wya, r_wya, s_end, r_end, s_n, r_n,
 ):
@@ -288,13 +288,17 @@
     def w_part(h, k):
         return pl.ds(pl.multiple_of(h * COLS + ((z + k) % NZ) * w_rows, 8), w_rows)
 
+    opposite_first = (2, 1, 3)
+
     def w_y(h):
         rows = w_half(h)
-        return (
-            make(wp.at[(y + 2) % NY, rows, :], wyrcv.at[0, rows, :], s_wy.at[h, 0], r_wy.at[h, 0], on_y(s)),
-            make(wp.at[(y - s + NY) % NY, rows, :], wyrcv.at[1, rows, :], s_wy.at[h, 1], r_wy.at[h, 1], on_y(-s)),
-            make(wcomb.at[rows, :], wyrcv.at[2, rows, :], s_wy.at[h, 2], r_wy.at[h, 2], on_y(s)),
-        )
+        return [
+            make(
+                wp.at[(y + k) % NY, rows, :], wyrcv.at[k - 1, rows, :],
+                s_wy.at[h, k - 1], r_wy.at[h, k - 1], on_y(k),
+            )
+            for k in opposite_first
+        ]
 
     def w_z(h):
         return [
@@ -308,46 +312,37 @@
 
     def w_back_y(h):
         here = wfull.at[y, w_half(h), :]
-        other = wfull.at[(y - s + NY) % NY, w_half(h), :]
-        return (
-            make(here, here, s_wya.at[h, 0], r_wya.at[h, 0], on_y(s)),
-            make(here, here, s_wya.at[h, 1], r_wya.at[h, 1], on_y(-s)),
-            make(other, other, s_wya.at[h, 2], r_wya.at[h, 2], on_y(s)),
-        )
-
-    def w_stage(stage, h):
+        return [
+            make(here, here, s_wya.at[h, k - 1], r_wya.at[h, k - 1], on_y(k)) for k in opposite_first
+        ]
+
+    def w_to_z(h):
         rows = w_half(h)
-        if stage == 1:
-            _, _, relay = w_y(h)
-            w_y(h)[0].wait_recv()
-            wcomb[rows, :] = wp[(y + s + NY) % NY, rows, :] + wyrcv[0, rows, :]
-            relay.start()
-        if stage == 2:
-            for copy in w_y(h)[1:]:
-                copy.wait_recv()
-            wy[rows, :] = wp[y, rows, :] + wyrcv[1, rows, :] + wyrcv[2, rows, :]
-            for copy in w_z(h):
-                copy.start()
-        if stage == 3:
-            for copy in w_z(h):
-                copy.wait_recv()
-            total = wy[w_part(h, 0), :]
-            for k in range(NZ - 1):
-                total = total + wzrcv[h, k]
-            wfull[y, w_part(h, 0), :] = total
-            for copy in w_back_z(h):
-                copy.start()
-        if stage == 4:
-            for copy in w_back_z(h):
-                copy.wait_recv()
-            for copy in w_back_y(h)[:2]:
-                copy.start()
-        if stage == 5:
-            w_back_y(h)[0].wait_recv()
-            w_back_y(h)[2].start()
-        if stage == 6:
-            for copy in w_back_y(h)[1:]:
-                copy.wait_recv()
+        for copy in w_y(h):
+            copy.wait_recv()
+        wy[rows, :] = wp[y, rows, :] + wyrcv[0, rows, :] + wyrcv[1, rows, :] + wyrcv[2, rows, :]
+        for copy in w_z(h):
+            copy.start()
+
+    def w_from_z(h):
+        for copy in w_z(h):
+            copy.wait_recv()
+        total = wy[w_part(h, 0), :]
+        for k in range(NZ - 1):
+            total = total + wzrcv[h, k]
+        wfull[y, w_part(h, 0), :] = total
+        for copy in w_back_z(h):
+            copy.start()
+
+    def w_to_y(h):
+        for copy in w_back_z(h):
+            copy.wait_recv()
+        for copy in w_back_y(h):
+            copy.start()
+
+    def w_end(h):
+        for copy in w_back_y(h):
+            copy.wait_recv()
 
     g = dot6(pfull[x], pfull[x], 0, 0)
     for h in range(2):
@@ -368,11 +363,11 @@
     g0 = gram_y(0, first, g0)
     far.wait_recv()
     cb.wait_recv()
-    for n, k in enumerate((2, NY - s, NY + s, 0)):
+    for n, k in enumerate((*opposite_first, 0)):
         b = (y + k) % NY
         for h in range(2):
             wp[b, w_half(h), :] = dot3(b2[h], pfull[b], 1, 0)
-            if n < 2:
+            if n < 3:
                 w_y(h)[n].start()
     g0 = gram_gather_z(0, first, g0)
     g1 = gram_y(1, rest, g1)
@@ -394,13 +389,16 @@
             copy.start()
 
     gram_gather_z(1, rest, g1)
-    w_stage(1, 0)
+    w_to_z(0)
 
     @pl.when(x != 0)
     def _():
         for copy in diagonals():
             copy.start()
         diagonal_from(0).wait_recv()
+
+    def span(i, j):
+        return slice(i * BLK, j * BLK)
 
     def rest_x():
         here = gfull.at[x, rest]
@@ -411,9 +409,20 @@
             make(other, other, s_gx.at[2], r_gx.at[2], on_x(s)),
         )
 
+    def early():
+        here = gfull.at[0, pl.ds(2, 2)]
+        return [make(here, g10, s_gx.at[k + 5], r_gx.at[k + 5], on_x(k)) for k in (1, 3, 2)]
+
     def rest_near():
         for copy in gram_back_z(1, rest):
             copy.wait_recv()
+
+        @pl.when(x == 0)
+        def _():
+            for copy in early():
+                copy.start()
+            g10[...] = gfull[0, 2:4]
+
         for copy in rest_x()[:2]:
             copy.start()
 
@@ -421,29 +430,44 @@
         rest_x()[0].wait_recv()
         rest_x()[2].start()
 
+    def diagonal_end(chip):
+        @pl.when(x != chip)
+        def _():
+            diagonal_from(chip).wait_recv()
+
+    def early_end():
+        @pl.when(x != 0)
+        def _():
+            here = gfull.at[0, pl.ds(2, 2)]
+            make(here, g10, s_gx.at[x + 5], r_gx.at[x + 5], on_x(x)).wait_recv()
+
     def rest_end():
-        for chip in range(1, NX):
-
-            @pl.when(x != chip)
-            def _(chip=chip):
-                diagonal_from(chip).wait_recv()
-
+        diagonal_end(2)
+        diagonal_end(3)
         for copy in rest_x()[1:]:
             copy.wait_recv()
+        for i in range(2, 4):
+            for j in range(i + 1):
+                afac[span(i, i + 1), span(j, j + 1)] = load(i, j)
+        panel = dot6(afac[span(2, 4), span(0, 1)], xinv[span(0, 1), span(0, 1)], 1, 1)
+        afac[span(2, 4), span(0, 1)] = panel
+        afac[span(2, 4), span(1, 2)] = afac[span(2, 4), span(1, 2)] - dot6(
+            panel, afac[span(1, 2), span(0, 1)], 1, 1
+        )
 
     def let_go():
         for copy in pending:
             copy.wait_send()
         pending.clear()
 
-    def stage(n, h):
-        return functools.partial(w_stage, n, h)
+    def call(f, h):
+        return functools.partial(f, h)
 
     between = [
-        [(2, stage(1, 1)), (2, rest_near), (5, rest_far), (6, stage(2, 0))],
-        [(3, stage(3, 0)), (7, stage(3, 1))],
-        [(4, stage(4, 0)), (7, stage(4, 1))],
-        [(2, stage(5, 0)), (6, stage(5, 1))],
+        [(2, call(w_to_z, 1)), (2, rest_near), (5, rest_far)],
+        [(0, call(w_from_z, 0)), (4, call(w_from_z, 1)), (6, rest_end)],
+        [(2, call(w_to_y, 0)), (6, call(w_to_y, 1))],
+        [],
     ]
 
     def load(i, j):
@@ -458,10 +482,8 @@
     tril = lax.broadcasted_iota(jnp.int32, (BLK, BLK), 0) >= lax.broadcasted_iota(
         jnp.int32, (BLK, BLK), 1
     )
-    def span(i, j):
-        return slice(i * BLK, j * BLK)
-
     xinv[...] = jnp.zeros_like(xinv)
+    projected = jnp.concatenate([pfull[b] for b in range(4)], axis=1)
     mblk[...] = load(0, 0)
     for kb in range(4):
         here, below, done = span(kb, kb + 1), span(kb + 1, 4), span(0, kb + 1)
@@ -469,43 +491,28 @@
         inv = jnp.where(tril, iblk[...], 0.0)
         xinv[here, here] = inv
         if kb == 0:
-            w_stage(2, 1)
-            rest_end()
-            for i in range(1, 4):
-                for j in range(i + 1):
-                    afac[span(i, i + 1), span(j, j + 1)] = load(i, j)
-        if kb < 3:
+            early_end()
+            diagonal_end(1)
+            panel = dot6(g10[...].reshape(BLK, BLK), inv, 1, 1)
+            afac[span(1, 2), here] = panel
+            mblk[...] = load(1, 1) - dot6(panel, panel, 1, 1)
+        if kb == 1:
+            afac[below, here] = dot6(afac[below, here], inv, 1, 1)
+            left = afac[below, done]
+            mblk[...] = afac[span(2, 3), span(2, 3)] - dot6(left[:BLK], left[:BLK], 1, 1)
+            under = afac[span(3, 4), span(2, 4)] - dot6(left[BLK:], left, 1, 1)
+            afac[span(3, 4), span(2, 4)] = under
+        if kb == 2:
             panel = dot6(afac[below, here], inv, 1, 1)
             afac[below, here] = panel
-            mblk[...] = afac[span(kb + 1, kb + 2), span(kb + 1, kb + 2)] - dot6(
-                panel[:BLK], panel[:BLK], 1, 1
-            )
-            for j in range(kb + 1, 3):
-                under, column = span(j + 1, 4), span(j, j + 1)
-                at = (j - kb - 1) * BLK
-                afac[under, column] = afac[under, column] - dot6(
-                    panel[at + BLK :], panel[at : at + BLK], 1, 1
-                )
-                corner = span(j + 1, j + 2)
-                afac[corner, corner] = afac[corner, corner] - dot6(
-                    panel[at + BLK : at + 2 * BLK], panel[at + BLK : at + 2 * BLK], 1, 1
-                )
+            mblk[...] = afac[below, below] - dot6(panel, panel, 1, 1)
         if kb > 0:
             xinv[here, span(0, kb)] = -dot3(inv, mixed[:, span(0, kb)], 1, 0)
         if kb < 3:
             mixed[:, done] = dot3(afac[span(kb + 1, kb + 2), done], xinv[done, done], 1, 0)
+        qs[:, lanes(kb)] = dot3(projected[:, done], xinv[here, done], 1, 1)
         if kb == 1:
             let_go()
-    for h in range(2):
-        w_stage(6, h)
-    both = jnp.concatenate(
-        [jnp.concatenate([pfull[b], wfull[b]], axis=0) for b in range(4)], axis=1
-    )
-    for kb in range(4):
-        done = span(0, kb + 1)
-        result = dot3(both[:, done], xinv[span(kb, kb + 1), done], 1, 1)
-        qs[:, lanes(kb)] = result[:ROWS]
-        cs[:, lanes(kb)] = result[ROWS:]
     ends = [
         send(qs, q_hbm.at[c], s_end.at[0], r_end.at[0], pair),
         make(cs.at[half(o), :], c_hbm.at[c], s_end.at[1], r_end.at[1], pair),
@@ -516,6 +523,13 @@
         pltpu.make_async_copy(sq, n_hbm.at[c, x], out_sem.at[2]),
     ]
     stores[0].start()
+    for h in range(2):
+        w_end(h)
+        rows = w_half(h)
+        w = jnp.concatenate([wfull[b, rows, :] for b in range(4)], axis=1)
+        for kb in range(4):
+            done = span(0, kb + 1)
+            cs[rows, lanes(kb)] = dot3(w[:, done], xinv[span(kb, kb + 1), done], 1, 1)
     ends[1].start()
     stores[1].start()
     sq[...] = jnp.sum(cs[...] * cs[...], axis=0, keepdims=True)
@@ -529,6 +543,11 @@
     ]
     for copy in pending[:-len(sums)]:
         copy.wait_send()
+    @pl.when(x == 0)
+    def _():
+        for copy in early():
+            copy.wait_send()
+
     for copy in diagonals() + list(rest_x()) + gram_back_z(0, first) + gram_back_z(1, rest):
         copy.wait_send()
     for h in range(2):
@@ -565,8 +584,8 @@
         vm((BLK, BLK), F32), vm((3, BLK, BLK), F32), vm(chunk, F32),
         vm((2, 64, BLK), F32),
         vm((4, 5, 64, BLK), F32), vm((7, 5, 8, BLK), F32), vm((5, 8, BLK), F32),
-        vm((3, 5, 8, BLK), F32), vm((5, 8, BLK), F32), vm((4, 5, 64, BLK), F32),
-        vm((4, 2 * COLS, BLK), F32), vm((2 * COLS, BLK), F32),
+        vm((3, 5, 8, BLK), F32), vm((5, 8, BLK), F32), vm((4, 5, 64, BLK), F32), vm((2, 64, BLK), F32),
+        vm((4, 2 * COLS, BLK), F32),
         vm((3, 2 * COLS, BLK), F32), vm((2 * COLS, BLK), F32),
         vm((2, 7, COLS // NZ, BLK), F32), vm((4, 2 * COLS, BLK), F32),
         vm((RANK, RANK), F32), vm((RANK, RANK), F32), vm((BLK, RANK), F32),
@@ -575,7 +594,7 @@
         vm((1, RANK), F32),
         pltpu.SemaphoreType.DMA((3,)),
     ]
-    for n in (2, 3, 3, (2, 7), (2, 3), 6, (2, 7), (2, 3), (2, 7), (2, 7), (2, 3), 2, 7):
+    for n in (2, 3, 3, (2, 7), (2, 3), 9, (2, 7), (2, 3), (2, 7), (2, 7), (2, 3), 2, 7):
         shape = n if isinstance(n, tuple) else (n,)
         scratch += [pltpu.SemaphoreType.DMA(shape), pltpu.SemaphoreType.DMA(shape)]
     hbm = pl.BlockSpec(memory_space=pl.ANY)

time: 71.1 us -> 70 us (0.985)
  Pallas kernels: 70.4 us -> 69.2 us
    pallas_call x1, Pallas kernels: 67.8 us -> 66.6 us  [on_device(): pl.pallas_call(kernel, out_shape=(jax.ShapeDtypeStruct((2, ROWS, RANK), F...]
where the time goes in v6:
time: 70 us; the launch traced here: 69.8 us
  Pallas kernels  69.2 us (99%)
    pallas_call x1, Pallas kernels, on_device(): pl.pallas_call(kernel, out_shape=(jax.ShapeDtypeStruct((2, ROWS, RANK), F...  66.6 us
    pallas_call x1, Pallas kernels, on_device(): pl.pallas_call(finish, grid=(2,), out_shape=(jax.ShapeDtypeStruct((2, COL...  2.61 us

profile of v6, /device:TPU:1, one launch (start us, length us, event | category | flops | bytes accessed | tf_op | source)
XLA Modules:
  0.0 69.8 jit_solution(9507780145017232135)
XLA Ops:
  0.6 66.6 %shard_map.58 = (f32[2,128,512]{2,1,0:T(8,128)}, f32[2,192,512]{2,1,0:T(8,128)}, f32[2,4,1,512]{3,2,1,0:T(1,128)}) custom-call(f32[2,192,128]{2,1,0:T(8,128)} %bitcast.4, bf16[2,192,128]{2,1,0:T(8,128)(2,1)} %bitcast.6, f32[2,192,512]{2,1,0:T(8,128)} %basis_hbm.1), custom_call_target="tpu_custom_call" | custom-call | tf_op jit(solution)/shard_map/pallas_call | solution.py:602
  67.2 2.6 %shard_map.59 = (f32[2,192,128]{2,1,0:T(8,128)}, f32[2,192,512]{2,1,0:T(8,128)}, bf16[2,192,128]{2,1,0:T(8,128)(2,1)}) custom-call(f32[2,192,128]{2,1,0:T(8,128)} %bitcast.5, bf16[2,192,128]{2,1,0:T(8,128)(2,1)} %bitcast.7, f32[2,128,512]{2,1,0:T(8,128)} %get-tuple-element.9.q_ref, f32[2,192,512]{2,1,0:T(8,128)} %get-tuple-element.10.c_ref, ...), custom_call_target="tpu_custom_call" | custom-call | tf_op jit(solution)/shard_map/pallas_call | solution.py:620

commit v7 on v6

--- a/solution.py
+++ b/solution.py
@@ -389,7 +389,6 @@
             copy.start()
 
     gram_gather_z(1, rest, g1)
-    w_to_z(0)
 
     @pl.when(x != 0)
     def _():
@@ -464,9 +463,9 @@
         return functools.partial(f, h)
 
     between = [
-        [(2, call(w_to_z, 1)), (2, rest_near), (5, rest_far)],
-        [(0, call(w_from_z, 0)), (4, call(w_from_z, 1)), (6, rest_end)],
-        [(2, call(w_to_y, 0)), (6, call(w_to_y, 1))],
+        [(2, call(w_to_z, 0)), (4, rest_near), (5, call(w_to_z, 1)), (7, rest_far)],
+        [(2, call(w_from_z, 0)), (5, call(w_from_z, 1)), (7, rest_end)],
+        [(3, call(w_to_y, 0)), (6, call(w_to_y, 1))],
         [],
     ]
 

time: 70 us -> 69.3 us (0.990)
  no operation moved by 1% of the time
where the time goes in v7:
time: 69.3 us; the launch traced here: 69.2 us
  Pallas kernels  68.6 us (99%)
    pallas_call x1, Pallas kernels, on_device(): pl.pallas_call(kernel, out_shape=(jax.ShapeDtypeStruct((2, ROWS, RANK), F...  65.9 us
    pallas_call x1, Pallas kernels, on_device(): pl.pallas_call(finish, grid=(2,), out_shape=(jax.ShapeDtypeStruct((2, COL...  2.61 us

profile of v7, /device:TPU:1, one launch (start us, length us, event | category | flops | bytes accessed | tf_op | source)
XLA Modules:
  0.0 69.2 jit_solution(17617215790639874564)
XLA Ops:
  0.6 65.9 %shard_map.58 = (f32[2,128,512]{2,1,0:T(8,128)}, f32[2,192,512]{2,1,0:T(8,128)}, f32[2,4,1,512]{3,2,1,0:T(1,128)}) custom-call(f32[2,192,128]{2,1,0:T(8,128)} %bitcast.4, bf16[2,192,128]{2,1,0:T(8,128)(2,1)} %bitcast.6, f32[2,192,512]{2,1,0:T(8,128)} %basis_hbm.1), custom_call_target="tpu_custom_call" | custom-call | tf_op jit(solution)/shard_map/pallas_call | solution.py:601
  66.6 2.6 %shard_map.59 = (f32[2,192,128]{2,1,0:T(8,128)}, f32[2,192,512]{2,1,0:T(8,128)}, bf16[2,192,128]{2,1,0:T(8,128)(2,1)}) custom-call(f32[2,192,128]{2,1,0:T(8,128)} %bitcast.5, bf16[2,192,128]{2,1,0:T(8,128)(2,1)} %bitcast.7, f32[2,128,512]{2,1,0:T(8,128)} %get-tuple-element.9.q_ref, f32[2,192,512]{2,1,0:T(8,128)} %get-tuple-element.10.c_ref, ...), custom_call_target="tpu_custom_call" | custom-call | tf_op jit(solution)/shard_map/pallas_call | solution.py:619

commit v8 on v7

--- a/solution.py
+++ b/solution.py
@@ -45,87 +45,114 @@
     return one(ah, bh) + (one(ah, bl) + one(al, bh))
 
 
-def gram_long(a):
-    hi = a.astype(BF16).astype(F32)
-    rest = a - hi
-    mid = rest.astype(BF16).astype(F32)
-    low = rest - mid
-    lhs = jnp.concatenate([hi, hi, hi, mid, mid, low], axis=0).astype(BF16)
-    rhs = jnp.concatenate([hi, mid, low, hi, mid, hi], axis=0).astype(BF16)
+def dot_long(a, b):
+    def pieces(v):
+        hi = v.astype(BF16).astype(F32)
+        rest = v - hi
+        mid = rest.astype(BF16).astype(F32)
+        return hi, mid, rest - mid
+
+    a0, a1, a2 = pieces(a)
+    b0, b1, b2 = pieces(b)
+    lhs = jnp.concatenate([a0, a0, a0, a1, a1, a2], axis=0).astype(BF16)
+    rhs = jnp.concatenate([b0, b1, b2, b0, b1, b0], axis=0).astype(BF16)
     return lax.dot_general(lhs, rhs, (((0,), (0,)), ((), ())), preferred_element_type=F32)
 
 
-def invert_factor(m_ref, out_ref, prev, pan, between):
-    lane = lax.broadcasted_iota(jnp.int32, (NB, BLK), 1)
-    sub = lax.broadcasted_iota(jnp.int32, (NB, BLK), 0)
+def flat(a):
+    return a.reshape(NB, BLK)
+
+
+def tall(a):
+    return a.reshape(NB // 8, 8, BLK)
+
+
+def at_row(v, p):
+    return jnp.broadcast_to(v[p // 8, p % 8 : p % 8 + 1, :], (8, BLK))
+
+
+def at_rows(v, p):
+    return jnp.broadcast_to(
+        v[:, p // 8 : p // 8 + 1, p % 8 : p % 8 + 1, :], (v.shape[0], 1, 8, BLK)
+    )
+
+
+def at_lane(v, j):
+    return tall(jnp.broadcast_to(flat(v)[:, j : j + 1], (NB, BLK)))
+
+
+def rolled(v, shift):
+    return tall(pltpu.roll(flat(v), shift, 1))
+
+
+def invert_factor(m_ref, out_ref, pan, prev, between):
+    shape = (NB // 8, 8, BLK)
+    lane = lax.broadcasted_iota(jnp.int32, shape, 2)
+    sub = lax.broadcasted_iota(jnp.int32, shape, 0) * 8 + lax.broadcasted_iota(jnp.int32, shape, 1)
+    row_all = lax.broadcasted_iota(jnp.int32, (BLK, BLK), 0)
     lane_all = lax.broadcasted_iota(jnp.int32, (BLK, BLK), 1)
-    eye = lax.broadcasted_iota(jnp.int32, (BLK, BLK), 0) == lane_all
-    diagonal = jnp.where(eye, m_ref[...], 0.0)
+    block = m_ref[...]
+    diagonal = jnp.where(row_all == lane_all, block, 0.0)
     scale_row = lax.rsqrt(jnp.sum(diagonal, axis=0, keepdims=True))
     scale_col = lax.rsqrt(jnp.sum(diagonal, axis=1, keepdims=True))
-    scaled = m_ref[...] * scale_col * scale_row
+    scaled = pltpu.roll(block * scale_col * scale_row, NB, 1)
     m_ref[...] = scaled
-    pan[...] = scaled[:NB]
+    pan[...] = tall(scaled[:NB])
     prev[...] = jnp.zeros_like(prev)
-
-    def columns(rows, rel):
-        return [
-            jnp.broadcast_to(
-                jnp.sum(jnp.where(rel == j, rows, 0.0), axis=1, keepdims=True), (NB, BLK)
-            )
-            for j in range(NB)
-        ]
+    steps = BLK // NB
+    inside = lane < NB
 
     def step(b, carry):
         for at, call in between:
             pl.when(b == at)(call)
         r0 = pl.multiple_of(b * NB, NB)
         after = pl.multiple_of(jnp.minimum(r0 + NB, BLK - NB), NB)
-        rel = lane - r0
-        inside = jnp.logical_and(rel >= 0, rel < NB)
-        rel_all = lane_all - r0
-        inside_before = jnp.logical_and(rel_all >= -NB, rel_all < 0)
-
-        m_ref[...] = jnp.where(inside_before, 0.0, m_ref[...]) - gram_long(prev[...])
+        was = lane_all < jnp.where(b > 0, NB, 0)
+        update = dot_long(prev[0], prev[1])
+        m_ref[...] = pltpu.roll(jnp.where(was, 0.0, m_ref[...]) - update, BLK - NB, 1)
 
         rows = pan[...]
-        cols = jnp.stack(columns(rows, rel))
-        full = jnp.where(inside, jnp.where(rel == sub, 1.0, 0.0), rows)
+        cols = jnp.stack([at_lane(rows, NB + j) for j in range(NB)])
+        full = jnp.where(inside, jnp.where(lane == sub, 1.0, 0.0), rolled(rows, BLK - NB))
         lower = full
-        scale = jnp.zeros((NB, BLK), F32)
+        scale = jnp.zeros(shape, F32)
         for p in range(0, NB, 2):
             u1, u2 = cols[0], cols[1]
-            a, e, d = u1[p : p + 1], u2[p : p + 1], u2[p + 1 : p + 2]
+            a, e, d = at_row(u1, p), at_row(u2, p), at_row(u2, p + 1)
             det = a * d - e * e
             inv = pl.reciprocal(det, approx=True)
             inv = inv * (2.0 - det * inv)
             v1, v2 = d * u1 - e * u2, a * u2 - e * u1
-            ia = 1.0 / a
+            root = lax.rsqrt(a)
+            ia = root * root
             under = sub > p + 1
             w1, w2 = v1 * inv, v2 * inv
+            pivots1 = jnp.where(sub == p, 1.0 - d * inv, jnp.where(sub == p + 1, e * inv, w1))
+            pivots2 = jnp.where(sub == p, e * inv, jnp.where(sub == p + 1, 1.0 - a * inv, w2))
+            if p + 2 < NB:
+                rest = cols[2:]
+                cols = rest - (pivots1[None] * at_rows(rest, p) + pivots2[None] * at_rows(rest, p + 1))
+            full = full - (pivots1 * at_row(full, p) + pivots2 * at_row(full, p + 1))
             l1 = jnp.where(under, w1, jnp.where(sub == p + 1, e * ia, 0.0))
             l2 = jnp.where(under, w2, 0.0)
-            lower = lower - (l1 * lower[p : p + 1] + l2 * lower[p + 1 : p + 2])
-            scale = jnp.where(sub == p, lax.rsqrt(a), scale)
+            lower = lower - (l1 * at_row(lower, p) + l2 * at_row(lower, p + 1))
+            scale = jnp.where(sub == p, root, scale)
             scale = jnp.where(sub == p + 1, lax.rsqrt(det * ia), scale)
-            w1 = jnp.where(sub == p, 1.0 - d * inv, jnp.where(sub == p + 1, e * inv, w1))
-            w2 = jnp.where(sub == p, e * inv, jnp.where(sub == p + 1, 1.0 - a * inv, w2))
-            if p + 2 < NB:
-                rest = cols[2:]
-                cols = rest - (w1[None] * rest[:, p : p + 1] + w2[None] * rest[:, p + 1 : p + 2])
-            full = full - (w1 * full[p : p + 1] + w2 * full[p + 1 : p + 2])
-        lower = lower * scale
-        prev[...] = lower
-        out_ref[pl.ds(r0, NB), :] = lower * scale_row
-
-        rows = m_ref[pl.ds(after, NB), :]
-        terms = [m * full[j : j + 1] for j, m in enumerate(columns(rows, rel))]
+        lower = flat(lower * scale)
+        unturned = pltpu.roll(lower, r0, 1)
+        prev[0] = unturned
+        prev[1] = lower
+        out_ref[pl.ds(r0, NB), :] = unturned
+
+        old = tall(m_ref[pl.ds(after, NB), :])
+        terms = [at_lane(old, j) * at_row(full, j) for j in range(NB)]
         while len(terms) > 1:
             terms = [terms[i] + terms[i + 1] for i in range(0, len(terms), 2)]
-        pan[...] = jnp.where(inside, 0.0, rows) - terms[0]
+        pan[...] = jnp.where(inside, 0.0, old) - terms[0]
         return carry
 
-    lax.fori_loop(0, BLK // NB, step, 0)
+    lax.fori_loop(0, steps, step, 0)
+    out_ref[...] = jnp.where(row_all >= lane_all, out_ref[...] * scale_row, 0.0)
 
 
 def kernel(
@@ -486,7 +513,7 @@
     mblk[...] = load(0, 0)
     for kb in range(4):
         here, below, done = span(kb, kb + 1), span(kb + 1, 4), span(0, kb + 1)
-        invert_factor(mblk, iblk, prev, pan, between[kb])
+        invert_factor(mblk, iblk, pan, prev, between[kb])
         inv = jnp.where(tril, iblk[...], 0.0)
         xinv[here, here] = inv
         if kb == 0:
@@ -588,7 +615,7 @@
         vm((3, 2 * COLS, BLK), F32), vm((2 * COLS, BLK), F32),
         vm((2, 7, COLS // NZ, BLK), F32), vm((4, 2 * COLS, BLK), F32),
         vm((RANK, RANK), F32), vm((RANK, RANK), F32), vm((BLK, RANK), F32),
-        *[vm((BLK, BLK), F32)] * 2, *[vm((NB, BLK), F32)] * 2,
+        *[vm((BLK, BLK), F32)] * 2, vm((2, NB, BLK), F32), vm((NB // 8, 8, BLK), F32),
         vm((ROWS, RANK), F32), vm((2 * COLS, RANK), F32),
         vm((1, RANK), F32),
         pltpu.SemaphoreType.DMA((3,)),

time: 69.3 us -> 70.6 us (1.019)
  Pallas kernels: 68.6 us -> 69.8 us
    pallas_call x1, Pallas kernels: 65.9 us -> 67.2 us  [on_device(): pl.pallas_call(kernel, out_shape=(jax.ShapeDtypeStruct((2, ROWS, RANK), F...]
where the time goes in v8:
time: 70.6 us; the launch traced here: 70.4 us
  Pallas kernels  69.8 us (99%)
    pallas_call x1, Pallas kernels, on_device(): pl.pallas_call(kernel, out_shape=(jax.ShapeDtypeStruct((2, ROWS, RANK), F...  67.2 us
    pallas_call x1, Pallas kernels, on_device(): pl.pallas_call(finish, grid=(2,), out_shape=(jax.ShapeDtypeStruct((2, COL...  2.61 us

profile of v8, /device:TPU:1, one launch (start us, length us, event | category | flops | bytes accessed | tf_op | source)
XLA Modules:
  0.0 70.4 jit_solution(11797422158504119448)
XLA Ops:
  0.6 67.2 %shard_map.58 = (f32[2,128,512]{2,1,0:T(8,128)}, f32[2,192,512]{2,1,0:T(8,128)}, f32[2,4,1,512]{3,2,1,0:T(1,128)}) custom-call(f32[2,192,128]{2,1,0:T(8,128)} %bitcast.4, bf16[2,192,128]{2,1,0:T(8,128)(2,1)} %bitcast.6, f32[2,192,512]{2,1,0:T(8,128)} %basis_hbm.1), custom_call_target="tpu_custom_call" | custom-call | tf_op jit(solution)/shard_map/pallas_call | solution.py:628
  67.8 2.6 %shard_map.59 = (f32[2,192,128]{2,1,0:T(8,128)}, f32[2,192,512]{2,1,0:T(8,128)}, bf16[2,192,128]{2,1,0:T(8,128)(2,1)}) custom-call(f32[2,192,128]{2,1,0:T(8,128)} %bitcast.5, bf16[2,192,128]{2,1,0:T(8,128)(2,1)} %bitcast.7, f32[2,128,512]{2,1,0:T(8,128)} %get-tuple-element.9.q_ref, f32[2,192,512]{2,1,0:T(8,128)} %get-tuple-element.10.c_ref, ...), custom_call_target="tpu_custom_call" | custom-call | tf_op jit(solution)/shard_map/pallas_call | solution.py:646

commit v9 on v6

--- a/solution.py
+++ b/solution.py
@@ -55,7 +55,7 @@
     return lax.dot_general(lhs, rhs, (((0,), (0,)), ((), ())), preferred_element_type=F32)
 
 
-def invert_factor(m_ref, out_ref, prev, pan, between):
+def invert_factor(m_ref, out_ref, between):
     lane = lax.broadcasted_iota(jnp.int32, (NB, BLK), 1)
     sub = lax.broadcasted_iota(jnp.int32, (NB, BLK), 0)
     lane_all = lax.broadcasted_iota(jnp.int32, (BLK, BLK), 1)
@@ -65,8 +65,6 @@
     scale_col = lax.rsqrt(jnp.sum(diagonal, axis=1, keepdims=True))
     scaled = m_ref[...] * scale_col * scale_row
     m_ref[...] = scaled
-    pan[...] = scaled[:NB]
-    prev[...] = jnp.zeros_like(prev)
 
     def columns(rows, rel):
         return [
@@ -77,8 +75,7 @@
         ]
 
     def step(b, carry):
-        for at, call in between:
-            pl.when(b == at)(call)
+        rows, previous = carry
         r0 = pl.multiple_of(b * NB, NB)
         after = pl.multiple_of(jnp.minimum(r0 + NB, BLK - NB), NB)
         rel = lane - r0
@@ -86,9 +83,8 @@
         rel_all = lane_all - r0
         inside_before = jnp.logical_and(rel_all >= -NB, rel_all < 0)
 
-        m_ref[...] = jnp.where(inside_before, 0.0, m_ref[...]) - gram_long(prev[...])
-
-        rows = pan[...]
+        m_ref[...] = jnp.where(inside_before, 0.0, m_ref[...]) - gram_long(previous)
+
         cols = jnp.stack(columns(rows, rel))
         full = jnp.where(inside, jnp.where(rel == sub, 1.0, 0.0), rows)
         lower = full
@@ -115,23 +111,26 @@
                 cols = rest - (w1[None] * rest[:, p : p + 1] + w2[None] * rest[:, p + 1 : p + 2])
             full = full - (w1 * full[p : p + 1] + w2 * full[p + 1 : p + 2])
         lower = lower * scale
-        prev[...] = lower
         out_ref[pl.ds(r0, NB), :] = lower * scale_row
 
-        rows = m_ref[pl.ds(after, NB), :]
-        terms = [m * full[j : j + 1] for j, m in enumerate(columns(rows, rel))]
+        old = m_ref[pl.ds(after, NB), :]
+        terms = [m * full[j : j + 1] for j, m in enumerate(columns(old, rel))]
         while len(terms) > 1:
             terms = [terms[i] + terms[i + 1] for i in range(0, len(terms), 2)]
-        pan[...] = jnp.where(inside, 0.0, rows) - terms[0]
-        return carry
-
-    lax.fori_loop(0, BLK // NB, step, 0)
+        return jnp.where(inside, 0.0, old) - terms[0], lower
+
+    def two_steps(i, carry):
+        for at, call in between:
+            pl.when(2 * i == at)(call)
+        return step(2 * i + 1, step(2 * i, carry))
+
+    lax.fori_loop(0, BLK // NB // 2, two_steps, (scaled[:NB], jnp.zeros((NB, BLK), F32)))
 
 
 def kernel(
     mom_hbm, grad_hbm, basis_hbm, q_hbm, c_hbm, n_hbm,
     mom_ref, grad_ref, basis_ref, in_sem, b2, bsend, pown, poth, prcv, psum, pcomb, xrcv, pfull, halves, gp, zrcv, gz, yrcv, gown, gfull, g10,
-    wp, wyrcv, wy, wzrcv, wfull, afac, xinv, mixed, mblk, iblk, prev, pan, qs, cs, sq, out_sem,
+    wp, wyrcv, wy, wzrcv, wfull, afac, xinv, mixed, mblk, iblk, qs, cs, sq, out_sem,
     s_pair, r_pair, s_xr, r_xr, s_xa, r_xa, s_zr, r_zr, s_y, r_y, s_gx, r_gx, s_gz, r_gz,
     s_wy, r_wy, s_wz, r_wz, s_wza, r_wza, s_wya, r_wya, s_end, r_end, s_n, r_n,
 ):
@@ -389,7 +388,6 @@
             copy.start()
 
     gram_gather_z(1, rest, g1)
-    w_to_z(0)
 
     @pl.when(x != 0)
     def _():
@@ -464,8 +462,8 @@
         return functools.partial(f, h)
 
     between = [
-        [(2, call(w_to_z, 1)), (2, rest_near), (5, rest_far)],
-        [(0, call(w_from_z, 0)), (4, call(w_from_z, 1)), (6, rest_end)],
+        [(2, call(w_to_z, 0)), (4, rest_near), (4, call(w_to_z, 1)), (6, rest_far)],
+        [(2, call(w_from_z, 0)), (4, call(w_from_z, 1)), (6, rest_end)],
         [(2, call(w_to_y, 0)), (6, call(w_to_y, 1))],
         [],
     ]
@@ -487,7 +485,7 @@
     mblk[...] = load(0, 0)
     for kb in range(4):
         here, below, done = span(kb, kb + 1), span(kb + 1, 4), span(0, kb + 1)
-        invert_factor(mblk, iblk, prev, pan, between[kb])
+        invert_factor(mblk, iblk, between[kb])
         inv = jnp.where(tril, iblk[...], 0.0)
         xinv[here, here] = inv
         if kb == 0:
@@ -589,7 +587,7 @@
         vm((3, 2 * COLS, BLK), F32), vm((2 * COLS, BLK), F32),
         vm((2, 7, COLS // NZ, BLK), F32), vm((4, 2 * COLS, BLK), F32),
         vm((RANK, RANK), F32), vm((RANK, RANK), F32), vm((BLK, RANK), F32),
-        *[vm((BLK, BLK), F32)] * 2, *[vm((NB, BLK), F32)] * 2,
+        *[vm((BLK, BLK), F32)] * 2,
         vm((ROWS, RANK), F32), vm((2 * COLS, RANK), F32),
         vm((1, RANK), F32),
         pltpu.SemaphoreType.DMA((3,)),

time: 70 us -> 69.9 us (level)
  no operation moved by 1% of the time
where the time goes in v9:
time: 69.9 us; the launch traced here: 69.8 us
  Pallas kernels  69.2 us (99%)
    pallas_call x1, Pallas kernels, on_device(): pl.pallas_call(kernel, out_shape=(jax.ShapeDtypeStruct((2, ROWS, RANK), F...  66.6 us
    pallas_call x1, Pallas kernels, on_device(): pl.pallas_call(finish, grid=(2,), out_shape=(jax.ShapeDtypeStruct((2, COL...  2.61 us

profile of v9, /device:TPU:1, one launch (start us, length us, event | category | flops | bytes accessed | tf_op | source)
XLA Modules:
  0.0 69.8 jit_solution(7888490065806208285)
XLA Ops:
  0.6 66.6 %shard_map.58 = (f32[2,128,512]{2,1,0:T(8,128)}, f32[2,192,512]{2,1,0:T(8,128)}, f32[2,4,1,512]{3,2,1,0:T(1,128)}) custom-call(f32[2,192,128]{2,1,0:T(8,128)} %bitcast.4, bf16[2,192,128]{2,1,0:T(8,128)(2,1)} %bitcast.6, f32[2,192,512]{2,1,0:T(8,128)} %basis_hbm.1), custom_call_target="tpu_custom_call" | custom-call | tf_op jit(solution)/shard_map/pallas_call | solution.py:600
  67.2 2.6 %shard_map.59 = (f32[2,192,128]{2,1,0:T(8,128)}, f32[2,192,512]{2,1,0:T(8,128)}, bf16[2,192,128]{2,1,0:T(8,128)(2,1)}) custom-call(f32[2,192,128]{2,1,0:T(8,128)} %bitcast.5, bf16[2,192,128]{2,1,0:T(8,128)(2,1)} %bitcast.7, f32[2,128,512]{2,1,0:T(8,128)} %get-tuple-element.9.q_ref, f32[2,192,512]{2,1,0:T(8,128)} %get-tuple-element.10.c_ref, ...), custom_call_target="tpu_custom_call" | custom-call | tf_op jit(solution)/shard_map/pallas_call | solution.py:618

commit v10 on v9

--- a/solution.py
+++ b/solution.py
@@ -15,7 +15,7 @@
 ROWS = 128
 COLS = 192
 BLK = 128
-NB = 16
+NB = 8
 F32 = jnp.float32
 BF16 = jnp.bfloat16
 HIGHEST = lax.Precision.HIGHEST
@@ -462,9 +462,9 @@
         return functools.partial(f, h)
 
     between = [
-        [(2, call(w_to_z, 0)), (4, rest_near), (4, call(w_to_z, 1)), (6, rest_far)],
-        [(2, call(w_from_z, 0)), (4, call(w_from_z, 1)), (6, rest_end)],
-        [(2, call(w_to_y, 0)), (6, call(w_to_y, 1))],
+        [(4, call(w_to_z, 0)), (8, rest_near), (10, call(w_to_z, 1)), (14, rest_far)],
+        [(4, call(w_from_z, 0)), (10, call(w_from_z, 1)), (14, rest_end)],
+        [(6, call(w_to_y, 0)), (12, call(w_to_y, 1))],
         [],
     ]
 

time: 69.9 us -> 70.7 us (1.011)
  Pallas kernels: 69.2 us -> 70 us
    pallas_call x1, Pallas kernels: 66.6 us -> 67.4 us  [on_device(): pl.pallas_call(kernel, out_shape=(jax.ShapeDtypeStruct((2, ROWS, RANK), F...]
where the time goes in v10:
time: 70.7 us; the launch traced here: 70.6 us
  Pallas kernels  70 us (99%)
    pallas_call x1, Pallas kernels, on_device(): pl.pallas_call(kernel, out_shape=(jax.ShapeDtypeStruct((2, ROWS, RANK), F...  67.4 us
    pallas_call x1, Pallas kernels, on_device(): pl.pallas_call(finish, grid=(2,), out_shape=(jax.ShapeDtypeStruct((2, COL...  2.61 us

profile of v10, /device:TPU:1, one launch (start us, length us, event | category | flops | bytes accessed | tf_op | source)
XLA Modules:
  0.0 70.6 jit_solution(17098387470695905439)
XLA Ops:
  0.6 67.4 %shard_map.58 = (f32[2,128,512]{2,1,0:T(8,128)}, f32[2,192,512]{2,1,0:T(8,128)}, f32[2,4,1,512]{3,2,1,0:T(1,128)}) custom-call(f32[2,192,128]{2,1,0:T(8,128)} %bitcast.4, bf16[2,192,128]{2,1,0:T(8,128)(2,1)} %bitcast.6, f32[2,192,512]{2,1,0:T(8,128)} %basis_hbm.1), custom_call_target="tpu_custom_call" | custom-call | tf_op jit(solution)/shard_map/pallas_call | solution.py:600
  68.0 2.6 %shard_map.59 = (f32[2,192,128]{2,1,0:T(8,128)}, f32[2,192,512]{2,1,0:T(8,128)}, bf16[2,192,128]{2,1,0:T(8,128)(2,1)}) custom-call(f32[2,192,128]{2,1,0:T(8,128)} %bitcast.5, bf16[2,192,128]{2,1,0:T(8,128)(2,1)} %bitcast.7, f32[2,128,512]{2,1,0:T(8,128)} %get-tuple-element.9.q_ref, f32[2,192,512]{2,1,0:T(8,128)} %get-tuple-element.10.c_ref, ...), custom_call_target="tpu_custom_call" | custom-call | tf_op jit(solution)/shard_map/pallas_call | solution.py:618

commit v11 on v7

--- a/solution.py
+++ b/solution.py
@@ -191,7 +191,7 @@
     for load in loads[:3]:
         load.wait()
     bsend[...] = mom_ref[o] + grad_ref[o].astype(F32)
-    p = dot3(bsend[...], basis_ref[o], 0, 0)
+    p = dot3(bsend[...].T, basis_ref[o], 1, 0)
     for b in range(4):
         poth[b] = p[:, b * BLK : (b + 1) * BLK]
     pl.semaphore_wait(barrier, len(peers))
@@ -200,7 +200,7 @@
     own = mom_ref[c] + grad_ref[c].astype(F32)
     b2[c] = own
     loads[3].wait()
-    p = dot3(own, basis_ref[c], 0, 0)
+    p = dot3(own.T, basis_ref[c], 1, 0)
     for b in range(4):
         pown[b] = p[:, b * BLK : (b + 1) * BLK]
     cp.wait_recv()
@@ -344,18 +344,18 @@
         for copy in w_back_y(h):
             copy.wait_recv()
 
-    g = dot6(pfull[x], pfull[x], 0, 0)
+    g = dot6(pfull[x].T, pfull[x], 1, 0)
     for h in range(2):
         gp[x, h] = g[h * 64 : (h + 1) * 64]
     g0 = gram_z(0, first)
     across[0].wait_recv()
     far = gather_relay(across, *a_args)[1]
     across[1].wait_recv()
-    g = dot6(pfull[x + 1 - x // 3], pfull[x % 3], 0, 0)
+    g = dot6(pfull[x + 1 - x // 3].T, pfull[x % 3], 1, 0)
     for h in range(2):
         gp[x, 2 + h] = g[h * 64 : (h + 1) * 64]
     between_two = (x + 1) % 2
-    g = dot6(pfull[between_two + 2], pfull[between_two], 0, 0)
+    g = dot6(pfull[between_two + 2].T, pfull[between_two], 1, 0)
     for h in range(2):
         halves[h] = g[h * 64 : (h + 1) * 64]
     gp[x, 4] = halves[x // 2]
@@ -613,19 +613,22 @@
         ),
     )(momentum, grad, basis)
 
-    def one(*shape):
-        return pl.BlockSpec((1, *shape), lambda i: (i,) + (0,) * len(shape))
+    def whole(*shape):
+        return pl.BlockSpec((1, *shape), lambda i, j: (i,) + (0,) * len(shape))
+
+    def part(width):
+        return pl.BlockSpec((1, COLS // 2, width), lambda i, j: (i, j, 0))
 
     nm, nb, up = pl.pallas_call(
         finish,
-        grid=(2,),
+        grid=(2, 2),
         out_shape=(
             jax.ShapeDtypeStruct((2, COLS, ROWS), F32),
             jax.ShapeDtypeStruct((2, COLS, RANK), F32),
             jax.ShapeDtypeStruct((2, COLS, ROWS), BF16),
         ),
-        in_specs=[one(COLS, ROWS), one(COLS, ROWS), one(ROWS, RANK), one(COLS, RANK), one(NX, 1, RANK)],
-        out_specs=(one(COLS, ROWS), one(COLS, RANK), one(COLS, ROWS)),
+        in_specs=[part(ROWS), part(ROWS), whole(ROWS, RANK), part(RANK), whole(NX, 1, RANK)],
+        out_specs=(part(ROWS), part(RANK), part(ROWS)),
         compiler_params=pltpu.CompilerParams(vmem_limit_bytes=58 * 2**20),
     )(momentum, grad, q, coeffs, sums)
     return jnp.swapaxes(nm, 1, 2), nb, jnp.swapaxes(up, 1, 2)

time: 69.3 us -> 70.7 us (1.020)
  Pallas kernels: 68.6 us -> 69.9 us
    pallas_call x1, Pallas kernels: 2.61 us -> 3.96 us  [on_device(): pl.pallas_call(finish, grid=(2, 2), out_shape=(jax.ShapeDtypeStruct((2, C...]
where the time goes in v11:
time: 70.7 us; the launch traced here: 70.5 us
  Pallas kernels  69.9 us (99%)
    pallas_call x1, Pallas kernels, on_device(): pl.pallas_call(kernel, out_shape=(jax.ShapeDtypeStruct((2, ROWS, RANK), F...  65.9 us
    pallas_call x1, Pallas kernels, on_device(): pl.pallas_call(finish, grid=(2, 2), out_shape=(jax.ShapeDtypeStruct((2, C...  3.96 us

profile of v11, /device:TPU:1, one launch (start us, length us, event | category | flops | bytes accessed | tf_op | source)
XLA Modules:
  0.0 70.5 jit_solution(13133497392603558697)
XLA Ops:
  0.6 65.9 %shard_map.58 = (f32[2,128,512]{2,1,0:T(8,128)}, f32[2,192,512]{2,1,0:T(8,128)}, f32[2,4,1,512]{3,2,1,0:T(1,128)}) custom-call(f32[2,192,128]{2,1,0:T(8,128)} %bitcast.4, bf16[2,192,128]{2,1,0:T(8,128)(2,1)} %bitcast.6, f32[2,192,512]{2,1,0:T(8,128)} %basis_hbm.1), custom_call_target="tpu_custom_call" | custom-call | tf_op jit(solution)/shard_map/pallas_call | solution.py:601
  66.6 4.0 %shard_map.59 = (f32[2,192,128]{2,1,0:T(8,128)}, f32[2,192,512]{2,1,0:T(8,128)}, bf16[2,192,128]{2,1,0:T(8,128)(2,1)}) custom-call(f32[2,192,128]{2,1,0:T(8,128)} %bitcast.5, bf16[2,192,128]{2,1,0:T(8,128)(2,1)} %bitcast.7, f32[2,128,512]{2,1,0:T(8,128)} %get-tuple-element.9.q_ref, f32[2,192,512]{2,1,0:T(8,128)} %get-tuple-element.10.c_ref, ...), custom_call_target="tpu_custom_call" | custom-call | tf_op jit(solution)/shard_map/pallas_call | solution.py:622

commit v12 on v7

--- a/solution.py
+++ b/solution.py
@@ -561,15 +561,44 @@
         store.wait()
 
 
-def finish(mom_ref, grad_ref, q_ref, c_ref, n_ref, nm_ref, nb_ref, up_ref):
-    q, coeffs = q_ref[0], c_ref[0]
-    error = lax.dot_general(
-        coeffs.astype(BF16), q.astype(BF16), (((1,), (1,)), ((), ())), preferred_element_type=F32
-    )
-    nm_ref[0] = mom_ref[0] + grad_ref[0].astype(F32) - 0.05 * error
-    basis = coeffs * lax.rsqrt(n_ref[0, 0] + n_ref[0, 1] + n_ref[0, 2] + n_ref[0, 3] + 1e-06)
-    nb_ref[0] = basis
-    up_ref[0] = (math.sqrt(D * FF / RANK) * dot3(basis, q, 1, 1)).astype(BF16)
+def finish(
+    mom_hbm, grad_hbm, q_hbm, c_hbm, n_hbm, nm_hbm, nb_hbm, up_hbm,
+    mom_ref, grad_ref, q_ref, c_ref, n_ref, nm_ref, nb_ref, up_ref, in_sem, out_sem,
+):
+    pairs = ((c_hbm, c_ref), (n_hbm, n_ref), (q_hbm, q_ref), (mom_hbm, mom_ref), (grad_hbm, grad_ref))
+    loads = [
+        [pltpu.make_async_copy(src.at[m], dst.at[m], in_sem.at[m, i]) for i, (src, dst) in enumerate(pairs)]
+        for m in range(2)
+    ]
+    for copies in loads:
+        for copy in copies:
+            copy.start()
+    stores = []
+
+    def store(src, dst, m, i):
+        copy = pltpu.make_async_copy(src.at[m], dst.at[m], out_sem.at[m, i])
+        copy.start()
+        stores.append(copy)
+
+    for m in range(2):
+        for copy in loads[m][:2]:
+            copy.wait()
+        coeffs = c_ref[m]
+        basis = coeffs * lax.rsqrt(n_ref[m, 0] + n_ref[m, 1] + n_ref[m, 2] + n_ref[m, 3] + 1e-06)
+        nb_ref[m] = basis
+        store(nb_ref, nb_hbm, m, 0)
+        for copy in loads[m][2:]:
+            copy.wait()
+        q = q_ref[m]
+        error = lax.dot_general(
+            coeffs.astype(BF16), q.astype(BF16), (((1,), (1,)), ((), ())), preferred_element_type=F32
+        )
+        nm_ref[m] = mom_ref[m] + grad_ref[m].astype(F32) - 0.05 * error
+        store(nm_ref, nm_hbm, m, 1)
+        up_ref[m] = (math.sqrt(D * FF / RANK) * dot3(basis, q, 1, 1)).astype(BF16)
+        store(up_ref, up_hbm, m, 2)
+    for copy in stores:
+        copy.wait()
 
 
 def on_device(momentum, grad, basis):
@@ -613,19 +642,18 @@
         ),
     )(momentum, grad, basis)
 
-    def one(*shape):
-        return pl.BlockSpec((1, *shape), lambda i: (i,) + (0,) * len(shape))
-
+    shapes = (
+        jax.ShapeDtypeStruct((2, COLS, ROWS), F32),
+        jax.ShapeDtypeStruct((2, COLS, RANK), F32),
+        jax.ShapeDtypeStruct((2, COLS, ROWS), BF16),
+    )
     nm, nb, up = pl.pallas_call(
         finish,
-        grid=(2,),
-        out_shape=(
-            jax.ShapeDtypeStruct((2, COLS, ROWS), F32),
-            jax.ShapeDtypeStruct((2, COLS, RANK), F32),
-            jax.ShapeDtypeStruct((2, COLS, ROWS), BF16),
-        ),
-        in_specs=[one(COLS, ROWS), one(COLS, ROWS), one(ROWS, RANK), one(COLS, RANK), one(NX, 1, RANK)],
-        out_specs=(one(COLS, ROWS), one(COLS, RANK), one(COLS, ROWS)),
+        out_shape=shapes,
+        in_specs=[hbm] * 5,
+        out_specs=(hbm,) * 3,
+        scratch_shapes=[vm(v.shape, v.dtype) for v in (momentum, grad, q, coeffs, sums, *shapes)]
+        + [pltpu.SemaphoreType.DMA((2, 5)), pltpu.SemaphoreType.DMA((2, 3))],
         compiler_params=pltpu.CompilerParams(vmem_limit_bytes=58 * 2**20),
     )(momentum, grad, q, coeffs, sums)
     return jnp.swapaxes(nm, 1, 2), nb, jnp.swapaxes(up, 1, 2)

time: 69.3 us -> 69.8 us (level)
  no operation moved by 1% of the time
where the time goes in v12:
time: 69.8 us; the launch traced here: 69.6 us
  Pallas kernels  69 us (99%)
    pallas_call x1, Pallas kernels, on_device(): pl.pallas_call(kernel, out_shape=(jax.ShapeDtypeStruct((2, ROWS, RANK), F...  65.9 us
    pallas_call x1, Pallas kernels, on_device(): pl.pallas_call(finish, out_shape=shapes, in_specs=[hbm] * 5, out_specs=(h...  3.06 us

profile of v12, /device:TPU:1, one launch (start us, length us, event | category | flops | bytes accessed | tf_op | source)
XLA Modules:
  0.0 69.6 jit_solution(6660552281636908216)
XLA Ops:
  0.6 65.9 %shard_map.58 = (f32[2,128,512]{2,1,0:T(8,128)}, f32[2,192,512]{2,1,0:T(8,128)}, f32[2,4,1,512]{3,2,1,0:T(1,128)}) custom-call(f32[2,192,128]{2,1,0:T(8,128)} %bitcast.4, bf16[2,192,128]{2,1,0:T(8,128)(2,1)} %bitcast.6, f32[2,192,512]{2,1,0:T(8,128)} %basis_hbm.1), custom_call_target="tpu_custom_call" | custom-call | tf_op jit(solution)/shard_map/pallas_call | solution.py:630
  66.6 3.1 %shard_map.59 = (f32[2,192,128]{2,1,0:T(8,128)}, f32[2,192,512]{2,1,0:T(8,128)}, bf16[2,192,128]{2,1,0:T(8,128)(2,1)}) custom-call(f32[2,192,128]{2,1,0:T(8,128)} %bitcast.5, bf16[2,192,128]{2,1,0:T(8,128)(2,1)} %bitcast.7, f32[2,128,512]{2,1,0:T(8,128)} %get-tuple-element.9.q_hbm, f32[2,192,512]{2,1,0:T(8,128)} %get-tuple-element.10.c_hbm, ...), custom_call_target="tpu_custom_call" | custom-call | tf_op jit(solution)/shard_map/pallas_call | solution.py:650

commit v13 on v7

--- a/solution.py
+++ b/solution.py
@@ -463,9 +463,9 @@
         return functools.partial(f, h)
 
     between = [
-        [(2, call(w_to_z, 0)), (4, rest_near), (5, call(w_to_z, 1)), (7, rest_far)],
-        [(2, call(w_from_z, 0)), (5, call(w_from_z, 1)), (7, rest_end)],
-        [(3, call(w_to_y, 0)), (6, call(w_to_y, 1))],
+        [(3, call(w_to_z, 0)), (4, rest_near), (6, call(w_to_z, 1)), (7, rest_far)],
+        [(4, call(w_from_z, 0)), (6, call(w_from_z, 1)), (7, rest_end)],
+        [(4, call(w_to_y, 0)), (6, call(w_to_y, 1))],
         [],
     ]
 
@@ -562,14 +562,15 @@
 
 
 def finish(mom_ref, grad_ref, q_ref, c_ref, n_ref, nm_ref, nb_ref, up_ref):
-    q, coeffs = q_ref[0], c_ref[0]
-    error = lax.dot_general(
-        coeffs.astype(BF16), q.astype(BF16), (((1,), (1,)), ((), ())), preferred_element_type=F32
-    )
-    nm_ref[0] = mom_ref[0] + grad_ref[0].astype(F32) - 0.05 * error
-    basis = coeffs * lax.rsqrt(n_ref[0, 0] + n_ref[0, 1] + n_ref[0, 2] + n_ref[0, 3] + 1e-06)
-    nb_ref[0] = basis
-    up_ref[0] = (math.sqrt(D * FF / RANK) * dot3(basis, q, 1, 1)).astype(BF16)
+    for m in range(2):
+        q, coeffs = q_ref[m], c_ref[m]
+        error = lax.dot_general(
+            coeffs.astype(BF16), q.astype(BF16), (((1,), (1,)), ((), ())), preferred_element_type=F32
+        )
+        nm_ref[m] = mom_ref[m] + grad_ref[m].astype(F32) - 0.05 * error
+        basis = coeffs * lax.rsqrt(n_ref[m, 0] + n_ref[m, 1] + n_ref[m, 2] + n_ref[m, 3] + 1e-06)
+        nb_ref[m] = basis
+        up_ref[m] = (math.sqrt(D * FF / RANK) * dot3(basis, q, 1, 1)).astype(BF16)
 
 
 def on_device(momentum, grad, basis):
@@ -613,19 +614,19 @@
         ),
     )(momentum, grad, basis)
 
-    def one(*shape):
-        return pl.BlockSpec((1, *shape), lambda i: (i,) + (0,) * len(shape))
+    def both(*shape):
+        return pl.BlockSpec((2, *shape), lambda i: (0,) * (len(shape) + 1))
 
     nm, nb, up = pl.pallas_call(
         finish,
-        grid=(2,),
+        grid=(1,),
         out_shape=(
             jax.ShapeDtypeStruct((2, COLS, ROWS), F32),
             jax.ShapeDtypeStruct((2, COLS, RANK), F32),
             jax.ShapeDtypeStruct((2, COLS, ROWS), BF16),
         ),
-        in_specs=[one(COLS, ROWS), one(COLS, ROWS), one(ROWS, RANK), one(COLS, RANK), one(NX, 1, RANK)],
-        out_specs=(one(COLS, ROWS), one(COLS, RANK), one(COLS, ROWS)),
+        in_specs=[both(COLS, ROWS), both(COLS, ROWS), both(ROWS, RANK), both(COLS, RANK), both(NX, 1, RANK)],
+        out_specs=(both(COLS, ROWS), both(COLS, RANK), both(COLS, ROWS)),
         compiler_params=pltpu.CompilerParams(vmem_limit_bytes=58 * 2**20),
     )(momentum, grad, q, coeffs, sums)
     return jnp.swapaxes(nm, 1, 2), nb, jnp.swapaxes(up, 1, 2)

time: 69.3 us -> 69.7 us (level)
  no operation moved by 1% of the time
where the time goes in v13:
time: 69.7 us; the launch traced here: 69.6 us
  Pallas kernels  68.9 us (99%)
    pallas_call x1, Pallas kernels, on_device(): pl.pallas_call(kernel, out_shape=(jax.ShapeDtypeStruct((2, ROWS, RANK), F...  66.2 us
    pallas_call x1, Pallas kernels, on_device(): pl.pallas_call(finish, grid=(1,), out_shape=(jax.ShapeDtypeStruct((2, COL...  2.72 us

profile of v13, /device:TPU:1, one launch (start us, length us, event | category | flops | bytes accessed | tf_op | source)
XLA Modules:
  0.0 69.6 jit_solution(960158339690218877)
XLA Ops:
  0.6 66.2 %shard_map.58 = (f32[2,128,512]{2,1,0:T(8,128)}, f32[2,192,512]{2,1,0:T(8,128)}, f32[2,4,1,512]{3,2,1,0:T(1,128)}) custom-call(f32[2,192,128]{2,1,0:T(8,128)} %bitcast.4, bf16[2,192,128]{2,1,0:T(8,128)(2,1)} %bitcast.6, f32[2,192,512]{2,1,0:T(8,128)} %basis_hbm.1), custom_call_target="tpu_custom_call" | custom-call | tf_op jit(solution)/shard_map/pallas_call | solution.py:602
  66.8 2.7 %shard_map.59 = (f32[2,192,128]{2,1,0:T(8,128)}, f32[2,192,512]{2,1,0:T(8,128)}, bf16[2,192,128]{2,1,0:T(8,128)(2,1)}) custom-call(f32[2,192,128]{2,1,0:T(8,128)} %bitcast.5, bf16[2,192,128]{2,1,0:T(8,128)(2,1)} %bitcast.7, f32[2,128,512]{2,1,0:T(8,128)} %get-tuple-element.9.q_ref, f32[2,192,512]{2,1,0:T(8,128)} %get-tuple-element.10.c_ref, ...), custom_call_target="tpu_custom_call" | custom-call | tf_op jit(solution)/shard_map/pallas_call | solution.py:620

commit v14 on v7

--- a/solution.py
+++ b/solution.py
@@ -191,20 +191,23 @@
     for load in loads[:3]:
         load.wait()
     bsend[...] = mom_ref[o] + grad_ref[o].astype(F32)
-    p = dot3(bsend[...], basis_ref[o], 0, 0)
-    for b in range(4):
-        poth[b] = p[:, b * BLK : (b + 1) * BLK]
     pl.semaphore_wait(barrier, len(peers))
-    cp = send(poth, prcv, s_pair.at[0], r_pair.at[0], pair)
-    cb = send(bsend, b2.at[c], s_pair.at[1], r_pair.at[1], pair)
+    chunks = []
+    for k in (2, 1, 3, 0):
+        b = (x + k) % NX
+        at = pl.ds(pl.multiple_of(b * BLK, BLK), BLK)
+        poth[b] = dot3(bsend[...], basis_ref[o, :, at], 0, 0)
+        chunks.append(send(poth.at[b], prcv.at[b], s_pair.at[1 + k], r_pair.at[1 + k], pair))
+    cb = send(bsend, b2.at[c], s_pair.at[0], r_pair.at[0], pair)
     own = mom_ref[c] + grad_ref[c].astype(F32)
     b2[c] = own
     loads[3].wait()
     p = dot3(own, basis_ref[c], 0, 0)
     for b in range(4):
         pown[b] = p[:, b * BLK : (b + 1) * BLK]
-    cp.wait_recv()
-    for b in range(4):
+    for k, copy in zip((2, 1, 3, 0), chunks, strict=True):
+        copy.wait_recv()
+        b = (x + k) % NX
         psum[b] = pown[b] + prcv[b]
 
     def sum_start(parts, me, own, own_sem, rcv, rcv_sem, to):
@@ -593,7 +596,7 @@
         vm((1, RANK), F32),
         pltpu.SemaphoreType.DMA((3,)),
     ]
-    for n in (2, 3, 3, (2, 7), (2, 3), 9, (2, 7), (2, 3), (2, 7), (2, 7), (2, 3), 2, 7):
+    for n in (5, 3, 3, (2, 7), (2, 3), 9, (2, 7), (2, 3), (2, 7), (2, 7), (2, 3), 2, 7):
         shape = n if isinstance(n, tuple) else (n,)
         scratch += [pltpu.SemaphoreType.DMA(shape), pltpu.SemaphoreType.DMA(shape)]
     hbm = pl.BlockSpec(memory_space=pl.ANY)

time: 69.3 us -> 70.2 us (1.013)
  Pallas kernels: 68.6 us -> 69.4 us
    pallas_call x1, Pallas kernels: 65.9 us -> 66.8 us  [on_device(): pl.pallas_call(kernel, out_shape=(jax.ShapeDtypeStruct((2, ROWS, RANK), F...]
where the time goes in v14:
time: 70.2 us; the launch traced here: 70.1 us
  Pallas kernels  69.4 us (99%)
    pallas_call x1, Pallas kernels, on_device(): pl.pallas_call(kernel, out_shape=(jax.ShapeDtypeStruct((2, ROWS, RANK), F...  66.8 us
    pallas_call x1, Pallas kernels, on_device(): pl.pallas_call(finish, grid=(2,), out_shape=(jax.ShapeDtypeStruct((2, COL...  2.61 us

profile of v14, /device:TPU:1, one launch (start us, length us, event | category | flops | bytes accessed | tf_op | source)
XLA Modules:
  0.0 70.1 jit_solution(15882330124072263197)
XLA Ops:
  0.6 66.8 %shard_map.58 = (f32[2,128,512]{2,1,0:T(8,128)}, f32[2,192,512]{2,1,0:T(8,128)}, f32[2,4,1,512]{3,2,1,0:T(1,128)}) custom-call(f32[2,192,128]{2,1,0:T(8,128)} %bitcast.4, bf16[2,192,128]{2,1,0:T(8,128)(2,1)} %bitcast.6, f32[2,192,512]{2,1,0:T(8,128)} %basis_hbm.1), custom_call_target="tpu_custom_call" | custom-call | tf_op jit(solution)/shard_map/pallas_call | solution.py:604
  67.5 2.6 %shard_map.59 = (f32[2,192,128]{2,1,0:T(8,128)}, f32[2,192,512]{2,1,0:T(8,128)}, bf16[2,192,128]{2,1,0:T(8,128)(2,1)}) custom-call(f32[2,192,128]{2,1,0:T(8,128)} %bitcast.5, bf16[2,192,128]{2,1,0:T(8,128)(2,1)} %bitcast.7, f32[2,128,512]{2,1,0:T(8,128)} %get-tuple-element.9.q_ref, f32[2,192,512]{2,1,0:T(8,128)} %get-tuple-element.10.c_ref, ...), custom_call_target="tpu_custom_call" | custom-call | tf_op jit(solution)/shard_map/pallas_call | solution.py:622
